TPU v7x, 256 devices: a whole 4x4x8 slice. The times are simulated.
256 devices in a mesh: dp: 32 (over x, z), tensor: 8 (over y, core).
Axes of the slice: x: 4, y: 4, z: 8, core: 2. Of those that a mesh axis runs over, the one named last changes fastest.
Arguments:
- cand_q: bfloat16 [16384, 4096], P('dp', 'tensor'), may hold values from -6 to 6
- cand_k: bfloat16 [16384, 1024], P('dp', 'tensor'), may hold values from -6 to 6
- cand_v: bfloat16 [16384, 1024], P('dp', 'tensor'), may hold values from -6 to 6
- prompt_k: bfloat16 [32768, 1024], P('dp', 'tensor'), may hold values from -6 to 6
- prompt_v: bfloat16 [32768, 1024], P('dp', 'tensor'), may hold values from -6 to 6
- cand_group: int32 [512], P('dp'), may hold values from 0 to 31, as said below
- cand_len: int32 [512], P('dp'), may hold values from 8 to 32, as said below
- boundaries: int32 [512, 4], P('dp'), may hold values from 0 to 31, as said below
- residual: bfloat16 [16384, 8192], P(('dp', 'tensor')), may hold values from -3 to 3
- out_weight: bfloat16 [4096, 8192], P('tensor'), may hold values from -0.5 to 0.5
- head_weight: float32 [8192], replicated, may hold values from -0.0625 to 0.0625
Outputs:
- hidden_out: bfloat16 [16384, 8192], P(('dp', 'tensor'))
- rewards: float32 [512, 4], P(('dp', 'tensor'))
Inputs may be any that keep to these rules, and one draw needn't show every extreme that they name: `cand_group`: the candidates of one index of dp name each problem at most 2 times; in every draw one problem is named exactly 2 times by the candidates of every index of dp. `cand_len`: some candidate has length 32. A candidate's boundaries never fall and lie below its length; the last is its length minus one.
All inputs are finite; a program needn't handle non-finite values.
Results may differ from a plain program's by a relative error of at most 0.017.
Values may be sent and summed in bfloat16 or wider, within the bound.
A program may use at most 128 MiB of HBM per device.

v0:
```python
import math

import jax
import jax.numpy as jnp
from jax import lax
from jax.sharding import PartitionSpec as P

HD = 128
P_SIZE = 1024
L = 32


def soften(scores, value_rows, out_spec):
    highest = jnp.max(scores, axis=-1, keepdims=True)
    raised = jnp.exp(scores - highest)
    summed_exp = jnp.sum(raised, axis=-1, keepdims=True)
    shares = (raised / summed_exp).astype(jnp.bfloat16)
    mixed = jnp.einsum(out_spec, shares, value_rows, preferred_element_type=jnp.float32)
    return (mixed, (highest + jnp.log(summed_exp))[..., 0])


def attend_prompt(queries, prompt_keys, prompt_values, score_spec, out_spec):
    scores = jnp.einsum(score_spec, queries, prompt_keys, preferred_element_type=jnp.float32) * (
        1.0 / math.sqrt(HD)
    )
    return soften(scores, prompt_values, out_spec)


def merge_parts(prefix_out, prefix_lse, suffix_out, suffix_lse):
    largest = jnp.maximum(prefix_lse, suffix_lse)
    prefix_weight = jnp.exp(prefix_lse - largest)[..., None]
    suffix_weight = jnp.exp(suffix_lse - largest)[..., None]
    joined = prefix_weight * prefix_out.astype(jnp.float32) + suffix_weight * suffix_out
    return (joined / (prefix_weight + suffix_weight)).astype(jnp.bfloat16)


def local(
    cand_q,
    cand_k,
    cand_v,
    prompt_k,
    prompt_v,
    cand_group,
    cand_len,
    boundaries,
    residual,
    out_weight,
    head_weight,
):
    n_cand = cand_group.shape[0]
    q_cols = cand_q.shape[1]
    kv_cols = cand_k.shape[1]
    kv_local = kv_cols // HD
    group_ratio = q_cols // kv_cols
    queries = cand_q.reshape(n_cand, L, kv_local, group_ratio, HD)
    own_keys = cand_k.reshape(n_cand, L, kv_local, HD)
    own_values = cand_v.reshape(n_cand, L, kv_local, HD)
    causal = jnp.arange(L)[:, None] >= jnp.arange(L)[None, :]
    suffix_scores = jnp.einsum(
        "blkrd,bmkd->blkrm", queries, own_keys, preferred_element_type=jnp.float32
    ) * (1.0 / math.sqrt(HD))
    suffix_scores = jnp.where(causal[None, :, None, None, :], suffix_scores, -1e30)
    suffix_out, suffix_lse = soften(suffix_scores, own_values, "blkrm,bmkd->blkrd")
    cache_keys, cache_values = (
        lax.all_gather(prompt_k, "dp", axis=0, tiled=True),
        lax.all_gather(prompt_v, "dp", axis=0, tiled=True),
    )
    problems = cache_keys.shape[0] // P_SIZE
    chosen_keys = jnp.take(cache_keys.reshape(problems, P_SIZE, kv_local, HD), cand_group, axis=0)
    chosen_values = jnp.take(
        cache_values.reshape(problems, P_SIZE, kv_local, HD), cand_group, axis=0
    )
    prefix_out, prefix_lse = attend_prompt(
        queries, chosen_keys, chosen_values, "blkrd,bpkd->blkrp", "blkrp,bpkd->blkrd"
    )
    prefix_out = lax.optimization_barrier(prefix_out.astype(jnp.bfloat16))
    attention = merge_parts(prefix_out, prefix_lse, suffix_out, suffix_lse).reshape(
        n_cand * L, q_cols
    )
    pieces = lax.axis_size("tensor")
    rows_here = attention.shape[0] // pieces
    summed = lax.psum_scatter(
        jnp.dot(attention, out_weight, preferred_element_type=jnp.float32).astype(jnp.bfloat16),
        "tensor",
        scatter_dimension=0,
        tiled=True,
    ).astype(jnp.float32)
    tensor_index = lax.axis_index("tensor")
    local_rows = tensor_index * rows_here + jnp.arange(rows_here, dtype=jnp.int32)
    owner_cand = local_rows // L
    is_live = local_rows % L < jnp.take(cand_len, owner_cand, axis=0)
    hidden = residual.astype(jnp.float32) + summed
    hidden_out = jnp.where(is_live[:, None], hidden, 0.0).astype(jnp.bfloat16)
    per_piece = n_cand // pieces
    step_marks = lax.dynamic_slice_in_dim(boundaries, tensor_index * per_piece, per_piece, 0)
    row_index = (jnp.arange(per_piece, dtype=jnp.int32)[:, None] * L + step_marks).reshape(-1)
    picked = jnp.take(hidden_out, row_index, axis=0).astype(jnp.float32)
    normed = picked * lax.rsqrt(jnp.mean(picked * picked, axis=-1, keepdims=True) + 1e-06)
    logits = jnp.sum(normed * head_weight[None, :], axis=-1)
    rewards = jax.nn.sigmoid(logits).reshape(per_piece, step_marks.shape[1])
    return (hidden_out, rewards)


def solution(mesh):
    in_specs = (
        P("dp", "tensor"),
        P("dp", "tensor"),
        P("dp", "tensor"),
        P("dp", "tensor"),
        P("dp", "tensor"),
        P("dp"),
        P("dp"),
        P("dp", None),
        P(("dp", "tensor"), None),
        P("tensor", None),
        P(),
    )
    out_specs = (P(("dp", "tensor"), None), P(("dp", "tensor"), None))
    return jax.shard_map(local, mesh=mesh, in_specs=in_specs, out_specs=out_specs, check_vma=False)
```

profile of v0, /device:TPU:1, one launch (start us, length us, event | category | flops | bytes accessed | tf_op | source)
XLA Modules:
  0.0 299.6 jit_solution(9787795745834412830)
XLA Ops:
  7.2 0.0 all-gather.5.cloned.1.call-start
  7.2 0.7 all-gather.5.cloned.1.call-update
  7.9 0.0 all-gather.3.cloned.1.call-start
  8.0 0.7 all-gather.3.cloned.1.call-update
  8.7 0.0 reduce-scatter.2.cloned.1.call-start
  8.7 1.2 reshape.347
  9.9 0.7 compare_select_fusion
  10.6 1.8 fusion.50
  12.4 0.3 fusion.29
  12.7 0.7 compare_and_fusion
  13.3 99.0 %all-gather.5.cloned.1.call-done = bf16[32768,128]{1,0:T(8,128)(2,1)} async-done(((bf16[1024,128]{1,0:T(8,128)(2,1)}), bf16[32768,128]{1,0:T(8,128)(2,1)}) %all-gather.5.cloned.1.call-update) | async-done | bytes 8388624 | tf_op jit(solution)/shard_map/all_gather | solution.py:66
  112.3 6.4 %gather_fusion.3 = bf16[16,1024,128]{2,1,0:T(8,128)(2,1)} fusion(bf16[32,1024,128]{2,1,0:T(8,128)(2,1)} %bitcast.131, s32[1024]{0:T(1024)S(1)} %pad_clamp_fusion.1), kind=kCustom, calls=%fused_computation.1.clone | custom fusion | bytes 8388672 | tf_op jit(solution)/shard_map/jit(_take)/gather | solution.py:70
  118.7 91.6 %all-gather.3.cloned.1.call-done = bf16[32768,128]{1,0:T(8,128)(2,1)} async-done(((bf16[1024,128]{1,0:T(8,128)(2,1)}), bf16[32768,128]{1,0:T(8,128)(2,1)}) %all-gather.3.cloned.1.call-update) | async-done | bytes 8388624 | tf_op jit(solution)/shard_map/all_gather | solution.py:65
  210.3 6.4 %gather_fusion.2 = bf16[16,1024,128]{2,1,0:T(8,128)(2,1)} fusion(bf16[32,1024,128]{2,1,0:T(8,128)(2,1)} %bitcast.132, s32[1024]{0:T(1024)S(1)} %pad_clamp_fusion.1), kind=kCustom, calls=%fused_computation.clone | custom fusion | bytes 8388672 | tf_op jit(solution)/shard_map/jit(_take)/gather | solution.py:69
  216.8 4.0 %bitcast_reduce_fusion = (f32[16,32,4]{1,2,0:T(4,128)S(1)}, f32[16,1024,32,4]{1,2,3,0:T(8,128)S(1)}) fusion(bf16[16,32,4,128]{3,2,1,0:T(4,128)(2,1)S(1)} %reshape.347, bf16[16,1024,128]{2,1,0:T(8,128)(2,1)} %gather_fusion.2, pred[16]{0:T(512)(128)(4,1)S(1)} %compare_and_fusion), kind=kOutput, calls=%fused_computation.6 | convolution fusion | flops 543160320 | bytes 13115408 | tf_op jit(solution)/shard_map/blkrd,bpkd->blkrp/dot_general | solution.py:23
  220.7 1.9 fusion.1
  222.7 3.2 %fusion.24 = bf16[16,32,1,4,128]{4,1,3,0,2:T(8,128)(2,1)S(1)} fusion(f32[16,32,4]{1,2,0:T(4,128)S(1)} %fusion.1, f32[16,32,4]{1,2,0:T(4,128)S(1)} %get-tuple-element.6, f32[16,1024,32,4]{1,2,3,0:T(8,128)S(1)} %get-tuple-element.7, bf16[16,1024,128]{2,1,0:T(8,128)(2,1)S(1)} %copy-done.2, pred[16]{0:T(512)(128)(4,1)S(1)} %compare_and_fusion), kind=kOutput, calls=%fused_computation.33 | convolution fusion | flops 547618816 | bytes 13123600 | tf_op jit(solution)/shard_map/blkrp,bpkd->blkrd/dot_general | solution.py:18
  225.9 1.2 fusion.22
  227.1 0.3 copy.21
  227.4 10.1 %convolution_convert_fusion = bf16[512,8192]{1,0:T(8,128)(2,1)} fusion(bf16[512,8192]{1,0:T(8,128)(2,1)} %param.22, bf16[64,8,4,128]{3,2,1,0:T(4,128)(2,1)S(1)} %bitcast.133), kind=kOutput, calls=%fused_computation.4 | convolution fusion | flops 4299161600 | bytes 17301504 | tf_op jit(solution)/shard_map/dot_general | solution.py:83
  237.6 0.6 copy-done.6
  238.2 0.1 dynamic-slice_add_fusion
  238.3 0.1 copy.22
  238.4 0.1 reshape.356
  238.5 0.1 reshape.355
  238.6 0.8 gather_fusion
  239.4 50.3 %reduce-scatter.2.cloned.1.call-done = bf16[64,8192]{1,0:T(8,128)(2,1)} async-done(((bf16[512,8192]{1,0:T(8,128)(2,1)}), bf16[64,8192]{1,0:T(8,128)(2,1)}) %reduce-scatter.2.cloned.1.call-update) | async-done | bytes 1048592 | tf_op jit(solution)/shard_map/reduce_scatter | solution.py:82
  289.7 1.5 select_convert_fusion
  291.3 0.6 gather_fusion.1
  291.9 0.3 fusion.36
  292.2 0.3 fusion.38
  292.4 0.7 div.70
  (26 shorter events, 0.2 us)
Async XLA Ops:
  7.2 218.7 %copy-start = (bf16[512,128]{1,0:T(8,128)(2,1)S(1)}, bf16[512,128]{1,0:T(8,128)(2,1)}, u32[]{:S(2)}) copy-start(bf16[512,128]{1,0:T(8,128)(2,1)} %param.15) | copy-start | bytes 393220
  7.2 105.1 %all-gather.5.cloned.1.call-start = ((), (), s32[]{:S(2)}) async-start(), calls=%async_computation.2 | async-start | bytes 8650752 | tf_op jit(solution)/shard_map/all_gather | solution.py:66
  7.9 202.4 %all-gather.3.cloned.1.call-start = ((), (), s32[]{:S(2)}) async-start(), calls=%async_computation.1 | async-start | bytes 8650752 | tf_op jit(solution)/shard_map/all_gather | solution.py:65
  8.7 281.0 %reduce-scatter.2.cloned.1.call-start = ((), (), s32[]{:S(2)}) async-start(), calls=%async_computation.3 | async-start | bytes 9437184 | tf_op jit(solution)/shard_map/reduce_scatter | solution.py:82
  216.8 5.9 %copy-start.2 = (bf16[16,1024,128]{2,1,0:T(8,128)(2,1)S(1)}, bf16[16,1024,128]{2,1,0:T(8,128)(2,1)}, u32[]{:S(2)}) copy-start(bf16[16,1024,128]{2,1,0:T(8,128)(2,1)} %gather_fusion.3) | copy-start | bytes 12582916
  237.5 0.7 copy-start.6
  237.5 1.0 copy-start.1
  237.5 52.2 %copy-start.4 = (bf16[64,8192]{1,0:T(8,128)(2,1)S(1)}, bf16[64,8192]{1,0:T(8,128)(2,1)}, u32[]{:S(2)}) copy-start(bf16[64,8192]{1,0:T(8,128)(2,1)} %param.21) | copy-start | bytes 3145732
  237.5 54.6 %copy-start.5 = (f32[8192]{0:T(1024)S(1)}, f32[8192]{0:T(1024)}, u32[]{:S(2)}) copy-start(f32[8192]{0:T(1024)} %param.23) | copy-start | bytes 98308
  291.2 1.8 copy-start.3
Sparse Core Ops, SparseCore 0:
  10.6 101.6 all-gather.4
  114.9 95.3 all-gather.2
  237.7 51.9 reduce-scatter.1
where the time goes:
time: 300 us
  waiting for transfers between devices  242 us (81%)
  matrix products  20.3 us (7%)
  local copies, waits for them, and re-layouts  17.2 us (6%)
  between operations  13.9 us (5%)
  other arithmetic  5.78 us (2%)
    all_gather x1, waiting for transfers between devices, local(): lax.all_gather(prompt_v, 'dp', axis=0, tiled=True)  99 us
    all_gather x1, waiting for transfers between devices, local(): lax.all_gather(prompt_k, 'dp', axis=0, tiled=True)  91.6 us
    reduce_scatter x1, waiting for transfers between devices, local(): lax.psum_scatter(jnp.dot(attention, out_weight, preferred_element_type=jn...  50.3 us
    dot_general x1, matrix products, local(): jnp.dot(attention, out_weight, preferred_element_type=jnp.float32)  10.1 us
    gather x1, local copies, waits for them, and re-layouts, local(): jnp.take(cache_keys.reshape(problems, P_SIZE, kv_local, HD), cand_group,...  6.44 us
    gather x1, local copies, waits for them, and re-layouts, local(): jnp.take(cache_values.reshape(problems, P_SIZE, kv_local, HD), cand_group...  6.39 us
  transfers between devices with their start and end apart: 3, of which 3 were waited for; matrix products, arithmetic and copies ran while one was open for 4% of the time, Pallas kernels for 0%

commit v1 on v0

v1 whole, which is shorter than its diff:
```python
import functools
import math

import jax
import jax.numpy as jnp
from jax import lax
from jax.experimental import pallas as pl
from jax.experimental.pallas import tpu as pltpu
from jax.sharding import PartitionSpec as P

HD = 128
P_SIZE = 1024
L = 32
C = 16
PAIR = 2
R = 4
XN, ZN, YN = 4, 8, 4
D = 8192
SCALE = 1.0 / math.sqrt(HD)
LOG2E = 1.4426950408889634
TILE = 1024
TILES = D // TILE
F32 = jnp.float32
BF16 = jnp.bfloat16
VMEM_LIMIT = 56 * 1024 * 1024


def remote(src, dst, send_sem, recv_sem, device):
    return pltpu.make_async_remote_copy(
        src_ref=src,
        dst_ref=dst,
        send_sem=send_sem,
        recv_sem=recv_sem,
        device_id=device,
        device_id_type=pl.DeviceIdType.MESH,
    )


def barrier_with(devices):
    barrier = pltpu.get_barrier_semaphore()
    for device in devices:
        pl.semaphore_signal(
            barrier, inc=1, device_id=device, device_id_type=pl.DeviceIdType.MESH
        )
    pl.semaphore_wait(barrier, len(devices))


def rows_of(block):
    return jnp.concatenate([block[:, r * HD : (r + 1) * HD] for r in range(R)], axis=0)


def with_ones(values):
    return jnp.concatenate([values, jnp.ones(values.shape, values.dtype)], axis=1)


def soften(scores, value_rows):
    highest = jnp.max(scores, axis=-1, keepdims=True)
    raised = jnp.exp2((scores - highest) * (SCALE * LOG2E)).astype(BF16)
    mixed = jnp.dot(raised, with_ones(value_rows), preferred_element_type=F32)
    summed = mixed[:, HD:]
    return mixed[:, :HD] / summed, highest * SCALE + jnp.log(summed)


def scores_of(queries, keys):
    return lax.dot_general(
        queries, keys, (((1,), (1,)), ((), ())), preferred_element_type=F32
    )


def attend_kernel(
    group_s, q_in, ck, cv, pk, pv, attn,
    qbuf, kbuf, vbuf, tabv, tabs, res, lsb, rel_r, rel_l, sfo, sfl, slot_s,
    loc_sem, tab_ss, tab_rs, q_ss, q_rs, k_ss, k_rs, v_ss, v_rs,
    ret_ss, ret_rs, fwd_ss, fwd_rs, lse_ss, lse_rs,
):
    dp = lax.axis_index("dp")
    x, z = dp // ZN, dp % ZN
    xl = {"dp": ((x + XN - 1) % XN) * ZN + z}
    xr = {"dp": ((x + 1) % XN) * ZN + z}
    xx = {"dp": ((x + 2) % XN) * ZN + z}
    zl = {"dp": x * ZN + (z + ZN - 1) % ZN}
    zr = {"dp": x * ZN + (z + 1) % ZN}

    own_k = pltpu.make_async_copy(pk, kbuf.at[0], loc_sem.at[0])
    own_v = pltpu.make_async_copy(pv, vbuf.at[0], loc_sem.at[1])
    own_q = pltpu.make_async_copy(q_in, qbuf.at[pl.ds(0, C)], loc_sem.at[2])
    own_q.start()
    own_k.start()
    own_v.start()

    groups = [group_s[c] for c in range(C)]
    lane = lax.broadcasted_iota(jnp.int32, (8, 128), 1)
    table = jnp.zeros((8, 128), jnp.int32)
    for c in range(C):
        slot = jnp.int32(0)
        for e in range(c):
            slot = slot + jnp.where(groups[e] == groups[c], 1, 0)
        slot = jnp.minimum(slot, PAIR - 1)
        table = jnp.where(lane == groups[c] * PAIR + slot, c, table)
        away = (groups[c] // ZN - x + XN) % XN
        region = jnp.where(away == 0, 0, jnp.where(away == 3, 4, jnp.where(away == 1, 5, 6)))
        back = (z - groups[c] % ZN + ZN) % ZN
        order = jnp.where(back == 0, 0, jnp.where(back <= 4, 2 * back - 1, 2 * (ZN - back)))
        slot_s[c] = region * C + order * PAIR + slot
    tabv[0] = table

    barrier_with([zl, zr, xl, xr, xx])

    def k_to(n, src, device):
        return remote(src, kbuf.at[n], k_ss.at[n], k_rs.at[n], device)

    def v_to(n, src, device):
        return remote(src, vbuf.at[n], v_ss.at[n], v_rs.at[n], device)

    k_to(1, pk, zr).start()
    k_to(2, pk, zl).start()
    half = C // 2
    lo, hi = pl.ds(0, half), pl.ds(half, half)

    def q_copy(i, src, region, part, device):
        return remote(
            src, qbuf.at[pl.ds(region * C + part * half, half)], q_ss.at[i], q_rs.at[i], device
        )

    q_copies = [
        q_copy(0, q_in.at[lo], 1, 0, xr),
        q_copy(1, q_in.at[hi], 2, 1, xl),
        q_copy(2, q_in.at[hi], 1, 1, xr),
        q_copy(3, q_in.at[lo], 2, 0, xl),
        q_copy(4, qbuf.at[pl.ds(1 * C, half)], 3, 0, xr),
        q_copy(5, qbuf.at[pl.ds(2 * C + half, half)], 3, 1, xl),
    ]
    q_copies[0].start()
    q_copies[1].start()
    v_to(1, pv, zr).start()
    v_to(2, pv, zl).start()
    tab_copies = [
        remote(tabv.at[0], tabv.at[1], tab_ss.at[0], tab_rs.at[0], xr),
        remote(tabv.at[0], tabv.at[2], tab_ss.at[1], tab_rs.at[1], xl),
        remote(tabv.at[0], tabv.at[3], tab_ss.at[2], tab_rs.at[2], xx),
    ]
    for copy in tab_copies:
        copy.start()
    q_copies[2].start()
    q_copies[3].start()

    own_q.wait()
    row = lax.broadcasted_iota(jnp.int32, (4 * R * L, 4 * L), 0)
    col = lax.broadcasted_iota(jnp.int32, (4 * R * L, 4 * L), 1)
    allowed = (row // (R * L) == col // L) & (col % L <= row % L)

    def suffix(g, carry):
        queries = jnp.concatenate([rows_of(qbuf[g * 4 + k]) for k in range(4)], axis=0)
        keys = ck[pl.ds(g * 4 * L, 4 * L), :]
        scores = jnp.where(allowed, scores_of(queries, keys), -1e30)
        mixed, lse = soften(scores, cv[pl.ds(g * 4 * L, 4 * L), :])
        for k in range(4):
            sfo[g * 4 + k] = mixed[k * R * L : (k + 1) * R * L]
            sfl[g * 4 + k] = lse[k * R * L : (k + 1) * R * L]
        return carry

    lax.fori_loop(0, C // 4, suffix, 0)

    q_copies[0].wait_recv()
    q_copies[4].start()
    q_copies[1].wait_recv()
    q_copies[5].start()
    own_k.wait()
    own_v.wait()
    for n, device in ((1, zr), (2, zl)):
        k_to(n, kbuf.at[n], device).wait_recv()
        k_to(n + 2, kbuf.at[n], device).start()
    for n, device in ((1, zr), (2, zl)):
        v_to(n, vbuf.at[n], device).wait_recv()
        v_to(n + 2, vbuf.at[n], device).start()
    for copy in tab_copies:
        copy.wait_recv()
    to_smem = pltpu.make_async_copy(tabv, tabs, loc_sem.at[3])
    to_smem.start()
    for i in (2, 3, 4, 5):
        q_copies[i].wait_recv()
    to_smem.wait()

    eye = lax.broadcasted_iota(jnp.int32, (HD, HD), 0) == lax.broadcasted_iota(
        jnp.int32, (HD, HD), 1
    )

    def pair_at(region, n):
        return pl.ds(region * C + n * PAIR, PAIR)

    def one_at(region, n, u):
        return pl.ds(region * C + n * PAIR + u, 1)

    def returns(n):
        return (
            remote(res.at[pair_at(1, n)], res.at[pair_at(5, n)], ret_ss.at[0, n], ret_rs.at[0, n], xl),
            remote(res.at[pair_at(2, n)], res.at[pair_at(4, n)], ret_ss.at[1, n], ret_rs.at[1, n], xr),
            remote(res.at[one_at(3, n, 0)], rel_r.at[pl.ds(n, 1)], ret_ss.at[2, n], ret_rs.at[2, n], xr),
            remote(res.at[one_at(3, n, 1)], rel_l.at[pl.ds(n, 1)], ret_ss.at[3, n], ret_rs.at[3, n], xl),
        )

    def relays(n):
        return (
            remote(rel_r.at[pl.ds(n, 1)], res.at[one_at(6, n, 0)], fwd_ss.at[0, n], fwd_rs.at[0, n], xr),
            remote(rel_l.at[pl.ds(n, 1)], res.at[one_at(6, n, 1)], fwd_ss.at[1, n], fwd_rs.at[1, n], xl),
        )

    def relay(n):
        _, _, right, left = returns(n)
        on_right, on_left = relays(n)
        right.wait_recv()
        on_right.start()
        left.wait_recv()
        on_left.start()

    def step(n, carry):
        @pl.when(n == 2)
        def _():
            for m, device in ((3, zr), (4, zl)):
                k_to(m, kbuf.at[m], device).wait_recv()
                k_to(m + 2, kbuf.at[m], device).start()

        @pl.when(n == 3)
        def _():
            for m, device in ((3, zr), (4, zl)):
                v_to(m, vbuf.at[m], device).wait_recv()
                v_to(m + 2, vbuf.at[m], device).start()

        @pl.when(n == 5)
        def _():
            k_to(5, kbuf.at[5], zr).wait_recv()
            k_to(7, kbuf.at[5], zr).start()
            k_to(6, kbuf.at[6], zl).wait_recv()
            v_to(6, vbuf.at[6], zl).wait_recv()
            v_to(7, vbuf.at[6], zl).start()
            v_to(5, vbuf.at[5], zr).wait_recv()

        @pl.when(n == 7)
        def _():
            k_to(7, kbuf.at[5], zr).wait_recv()
            v_to(7, vbuf.at[6], zl).wait_recv()

        owner_z = (z + (1 - 2 * (n % 2)) * ((n + 1) // 2) + ZN) % ZN
        base = (x * ZN + owner_z) * PAIR

        def source(s, inner):
            queries = jnp.concatenate(
                [rows_of(qbuf[s * C + tabs[s, 0, base + u]]) for u in range(PAIR)], axis=0
            )
            mixed, lse = soften(scores_of(queries, kbuf[n]), vbuf[n])
            mixed = mixed.astype(BF16)
            for u in range(PAIR):
                at = s * C + n * PAIR + u
                for r in range(R):
                    first = (u * R + r) * L
                    res[at, :, r * HD : (r + 1) * HD] = mixed[first : first + L]
                lsb[at] = jnp.sum(
                    jnp.where(eye, lse[u * HD : (u + 1) * HD], 0.0), axis=0, keepdims=True
                )
            return inner

        lax.fori_loop(0, XN, source, 0)
        for copy in returns(n):
            copy.start()

        @pl.when(n >= 2)
        def _():
            relay(n - 2)

        return carry

    lax.fori_loop(0, ZN, step, 0)
    lse_copies = [
        remote(lsb.at[pl.ds(1 * C, C)], lsb.at[pl.ds(5 * C, C)], lse_ss.at[0], lse_rs.at[0], xl),
        remote(lsb.at[pl.ds(2 * C, C)], lsb.at[pl.ds(4 * C, C)], lse_ss.at[1], lse_rs.at[1], xr),
        remote(lsb.at[pl.ds(3 * C, C)], lsb.at[pl.ds(6 * C, C)], lse_ss.at[2], lse_rs.at[2], xx),
    ]
    for copy in lse_copies:
        copy.start()
    relay(ZN - 2)
    relay(ZN - 1)

    def arrived(n, carry):
        from_xl, from_xr, _, _ = returns(n)
        from_xl.wait_recv()
        from_xr.wait_recv()
        for copy in relays(n):
            copy.wait_recv()
        return carry

    lax.fori_loop(0, ZN, arrived, 0)
    for copy in lse_copies:
        copy.wait_recv()

    def merge(c, carry):
        at = slot_s[c]
        prefix = rows_of(res[at]).astype(F32)
        prefix_lse = jnp.sum(jnp.where(eye, lsb[at], 0.0), axis=1, keepdims=True)
        suffix_lse = sfl[c]
        largest = jnp.maximum(prefix_lse, suffix_lse)
        a = jnp.exp(prefix_lse - largest)
        b = jnp.exp(suffix_lse - largest)
        joined = ((a * prefix + b * sfo[c]) / (a + b)).astype(BF16)
        for r in range(R):
            attn[c, :, r * HD : (r + 1) * HD] = joined[r * L : (r + 1) * L]
        return carry

    lax.fori_loop(0, C, merge, 0)

    def sent(n, carry):
        for copy in returns(n) + relays(n):
            copy.wait_send()
        return carry

    lax.fori_loop(0, ZN, sent, 0)
    for copy in lse_copies + q_copies + tab_copies:
        copy.wait_send()
    for n in range(1, ZN):
        k_to(n, kbuf.at[0], zr).wait_send()
        v_to(n, vbuf.at[0], zr).wait_send()


def attend(group, q, ck, cv, pk, pv):
    dma = pltpu.SemaphoreType.DMA
    any_space = pl.BlockSpec(memory_space=pl.ANY)
    vmem = pl.BlockSpec(memory_space=pltpu.VMEM)
    smem = pl.BlockSpec(memory_space=pltpu.SMEM)
    return pl.pallas_call(
        attend_kernel,
        out_shape=jax.ShapeDtypeStruct((C, L, R * HD), BF16),
        in_specs=[smem, any_space, vmem, vmem, any_space, any_space],
        out_specs=vmem,
        scratch_shapes=[
            pltpu.VMEM((XN * C, L, R * HD), BF16),
            pltpu.VMEM((ZN, P_SIZE, HD), BF16),
            pltpu.VMEM((ZN, P_SIZE, HD), BF16),
            pltpu.VMEM((XN, 8, 128), jnp.int32),
            pltpu.SMEM((XN, 8, 128), jnp.int32),
            pltpu.VMEM((7 * C, L, R * HD), BF16),
            pltpu.VMEM((7 * C, 1, HD), F32),
            pltpu.VMEM((ZN, L, R * HD), BF16),
            pltpu.VMEM((ZN, L, R * HD), BF16),
            pltpu.VMEM((C, R * L, HD), F32),
            pltpu.VMEM((C, R * L, HD), F32),
            pltpu.SMEM((C,), jnp.int32),
            dma((4,)), dma((3,)), dma((3,)), dma((6,)), dma((6,)),
            dma((ZN,)), dma((ZN,)), dma((ZN,)), dma((ZN,)),
            dma((4, ZN)), dma((4, ZN)), dma((2, ZN)), dma((2, ZN)), dma((3,)), dma((3,)),
        ],
        compiler_params=pltpu.CompilerParams(
            collective_id=0, has_side_effects=True, vmem_limit_bytes=VMEM_LIMIT
        ),
        cost_estimate=pl.CostEstimate(
            flops=2 * 2 * 64 * 128 * P_SIZE * HD, bytes_accessed=8 << 20, transcendentals=8 << 20
        ),
    )(group, q, ck, cv, pk, pv)


def project_kernel(
    len_s, mark_s, attn, weight, residual, head_w, hidden, rewards,
    wbuf, send_a, recv_a, own, far_r, far_l, near_l, near_r, squares, dots,
    w_sem, a_ss, a_rs, far_ss, far_rs, now_ss, now_rs, late_ss, late_rs,
):
    t = lax.axis_index("tensor")
    y, core = t // 2, t % 2
    sibling = {"tensor": y * 2 + 1 - core}
    yr_at, yl_at, far_at = (y + 1) % YN, (y + YN - 1) % YN, (y + 2) % YN
    yr = {"tensor": yr_at * 2 + core}
    yl = {"tensor": yl_at * 2 + core}
    rows = C * L // (2 * YN)
    half = rows // 2
    lo, hi = pl.ds(0, half), pl.ds(half, half)

    def w_copy(i):
        return pltpu.make_async_copy(
            weight.at[:, pl.ds(pl.multiple_of(i * TILE, TILE), TILE)], wbuf.at[i], w_sem.at[i]
        )

    for i in range(TILES):
        w_copy(i).start()
    squares[...] = jnp.zeros_like(squares)
    dots[...] = jnp.zeros_like(dots)
    barrier_with([sibling, yl, yr])

    def a_copy(i):
        return remote(send_a.at[i], recv_a.at[i], a_ss.at[i], a_rs.at[i], sibling)

    def far_copies(i):
        return (
            remote(own.at[i, far_at, lo], far_r.at[i], far_ss.at[0, i], far_rs.at[0, i], yr),
            remote(own.at[i, far_at, hi], far_l.at[i], far_ss.at[1, i], far_rs.at[1, i], yl),
        )

    def now_copies(i):
        return (
            remote(own.at[i, yr_at, hi], near_l.at[i, hi], now_ss.at[0, i], now_rs.at[0, i], yr),
            remote(own.at[i, yl_at, lo], near_r.at[i, lo], now_ss.at[1, i], now_rs.at[1, i], yl),
        )

    def late_copies(i):
        return (
            remote(own.at[i, yr_at, lo], near_l.at[i, lo], late_ss.at[0, i], late_rs.at[0, i], yr),
            remote(own.at[i, yl_at, hi], near_r.at[i, hi], late_ss.at[1, i], late_rs.at[1, i], yl),
        )

    def multiply(i):
        w_copy(i).wait()
        for side, out in ((1 - core, send_a), (core, own)):
            left = attn[:, side].reshape(YN * rows, R * HD)
            part = jnp.dot(left, wbuf[i], preferred_element_type=F32)
            out[i] = part.astype(BF16).reshape(YN, rows, TILE)
        a_copy(i).start()

    def pair_sum(i):
        a_copy(i).wait_recv()
        own[i] = (own[i].astype(F32) + recv_a[i].astype(F32)).astype(BF16)
        for copy in far_copies(i) + now_copies(i):
            copy.start()

    def pass_on(i):
        to_r, to_l = far_copies(i)
        late_r, late_l = late_copies(i)
        to_r.wait_recv()
        own[i, yr_at, lo] = (own[i, yr_at, lo].astype(F32) + far_r[i].astype(F32)).astype(BF16)
        late_r.start()
        to_l.wait_recv()
        own[i, yl_at, hi] = (own[i, yl_at, hi].astype(F32) + far_l[i].astype(F32)).astype(BF16)
        late_l.start()

    row = lax.broadcasted_iota(jnp.int32, (rows, 1), 0)
    first = t * 2
    live = (row % L) < jnp.where(row < L, len_s[first], len_s[first + 1])

    def finish(i):
        for copy in now_copies(i) + late_copies(i):
            copy.wait_recv()
        at = pl.ds(pl.multiple_of(i * TILE, TILE), TILE)
        total = (
            residual[:, at].astype(F32)
            + own[i, y].astype(F32)
            + near_l[i].astype(F32)
            + near_r[i].astype(F32)
        )
        out = jnp.where(live, total, 0.0).astype(BF16)
        hidden[:, at] = out
        v = out.astype(F32)
        sq = v * v
        pr = v * head_w[:, at]
        squares[...] += functools.reduce(
            jnp.add, [sq[:, k * 128 : (k + 1) * 128] for k in range(TILE // 128)]
        )
        dots[...] += functools.reduce(
            jnp.add, [pr[:, k * 128 : (k + 1) * 128] for k in range(TILE // 128)]
        )

    def step(i, carry):
        @pl.when(i < TILES)
        def _():
            multiply(i)

        @pl.when((i >= 1) & (i < TILES + 1))
        def _():
            pair_sum(i - 1)

        @pl.when((i >= 2) & (i < TILES + 2))
        def _():
            pass_on(i - 2)

        @pl.when(i >= 3)
        def _():
            finish(i - 3)

        return carry

    lax.fori_loop(0, TILES + 3, step, 0)

    mean = jnp.sum(squares[...], axis=1, keepdims=True) * (1.0 / D)
    logit = jnp.sum(dots[...], axis=1, keepdims=True) * lax.rsqrt(mean + 1e-06)
    reward = 1.0 / (1.0 + jnp.exp(-logit))
    lane = lax.broadcasted_iota(jnp.int32, (1, 128), 1)
    wanted = jnp.full((1, 128), -1, jnp.int32)
    for k in range(8):
        wanted = jnp.where(lane == k, (k // 4) * L + mark_s[(first + k // 4) * 4 + k % 4], wanted)
    picked = jnp.where(row == wanted, reward, 0.0)
    rewards[...] = jnp.sum(picked, axis=0, keepdims=True)

    def sent(i, carry):
        a_copy(i).wait_send()
        for copy in far_copies(i) + now_copies(i) + late_copies(i):
            copy.wait_send()
        return carry

    lax.fori_loop(0, TILES, sent, 0)


def project(lens, marks, attn, weight, residual, head_w):
    dma = pltpu.SemaphoreType.DMA
    any_space = pl.BlockSpec(memory_space=pl.ANY)
    vmem = pl.BlockSpec(memory_space=pltpu.VMEM)
    smem = pl.BlockSpec(memory_space=pltpu.SMEM)
    rows = C * L // (2 * YN)
    return pl.pallas_call(
        project_kernel,
        out_shape=(
            jax.ShapeDtypeStruct((rows, D), BF16),
            jax.ShapeDtypeStruct((1, 128), F32),
        ),
        in_specs=[smem, smem, vmem, any_space, vmem, vmem],
        out_specs=(vmem, vmem),
        scratch_shapes=[
            pltpu.VMEM((TILES, R * HD, TILE), BF16),
            pltpu.VMEM((TILES, YN, rows, TILE), BF16),
            pltpu.VMEM((TILES, YN, rows, TILE), BF16),
            pltpu.VMEM((TILES, YN, rows, TILE), BF16),
            pltpu.VMEM((TILES, rows // 2, TILE), BF16),
            pltpu.VMEM((TILES, rows // 2, TILE), BF16),
            pltpu.VMEM((TILES, rows, TILE), BF16),
            pltpu.VMEM((TILES, rows, TILE), BF16),
            pltpu.VMEM((rows, 128), F32),
            pltpu.VMEM((rows, 128), F32),
            dma((TILES,)), dma((TILES,)), dma((TILES,)),
            dma((2, TILES)), dma((2, TILES)), dma((2, TILES)), dma((2, TILES)),
            dma((2, TILES)), dma((2, TILES)),
        ],
        compiler_params=pltpu.CompilerParams(
            collective_id=1, has_side_effects=True, vmem_limit_bytes=VMEM_LIMIT
        ),
        cost_estimate=pl.CostEstimate(
            flops=2 * C * L * R * HD * D, bytes_accessed=12 << 20, transcendentals=0
        ),
    )(lens, marks, attn, weight, residual, head_w)


def local(
    cand_q, cand_k, cand_v, prompt_k, prompt_v, cand_group, cand_len, boundaries,
    residual, out_weight, head_weight,
):
    attn = attend(
        cand_group, cand_q.reshape(C, L, R * HD), cand_k, cand_v, prompt_k, prompt_v
    )
    hidden, rewards = project(
        cand_len,
        boundaries.reshape(-1),
        attn.reshape(YN, 2, 2 * L, R * HD),
        out_weight,
        residual,
        head_weight.reshape(1, D),
    )
    return hidden, rewards[0, :8].reshape(2, 4)


def solution(mesh):
    in_specs = (
        P("dp", "tensor"),
        P("dp", "tensor"),
        P("dp", "tensor"),
        P("dp", "tensor"),
        P("dp", "tensor"),
        P("dp"),
        P("dp"),
        P("dp", None),
        P(("dp", "tensor"), None),
        P("tensor", None),
        P(),
    )
    out_specs = (P(("dp", "tensor"), None), P(("dp", "tensor"), None))
    return jax.shard_map(local, mesh=mesh, in_specs=in_specs, out_specs=out_specs, check_vma=False)
```

time: 300 us -> 121 us (0.40)
  waiting for transfers between devices: 242 us -> 0 us
  Pallas kernels: 0 us -> 115 us
  matrix products: 20.3 us -> 0 us
  between operations: 13.9 us -> 0.65 us
  local copies, waits for them, and re-layouts: 17.2 us -> 4.92 us
  other arithmetic: 5.78 us -> 0 us
    all_gather x2 -> x0, waiting for transfers between devices: 191 us -> none  [the longest x1 99 us: local(): lax.all_gather(prompt_v, 'dp', axis=0, tiled=True)]
    pallas_call x0 -> x2, Pallas kernels: none -> 115 us  [the longest x1 67.7 us: attend(): pl.pallas_call(attend_kernel, out_shape=jax.ShapeDtypeStruct((C, L, R * H...]
    reduce_scatter x1 -> x0, waiting for transfers between devices: 50.3 us -> none  [local(): lax.psum_scatter(jnp.dot(attention, out_weight, preferred_element_type=jn...]
    dot_general x5 -> x0, matrix products: 20.3 us -> none  [the longest x1 10.1 us: local(): jnp.dot(attention, out_weight, preferred_element_type=jnp.float32)]
    gather x4 -> x0, local copies, waits for them, and re-layouts: 14.2 us -> none  [the longest x1 6.44 us: local(): jnp.take(cache_keys.reshape(problems, P_SIZE, kv_local, HD), cand_group,...]
  transfers between devices with their start and end apart: 3 -> 0, of which waited for: 3 -> 0; matrix products, arithmetic and copies ran while one was open for 4% -> 0% of each run, Pallas kernels for 0% -> 0%
where the time goes in v1:
time: 121 us; the launch traced here: 120 us
  Pallas kernels  115 us (95%)
  local copies, waits for them, and re-layouts  4.92 us (4%)
    pallas_call x1, Pallas kernels, attend(): pl.pallas_call(attend_kernel, out_shape=jax.ShapeDtypeStruct((C, L, R * H...  67.7 us
    pallas_call x1, Pallas kernels, project(): pl.pallas_call(project_kernel, out_shape=(jax.ShapeDtypeStruct((rows, D),...  47.2 us
    unnamed x2, local copies, waits for them, and re-layouts  3.02 us

profile of v1, /device:TPU:1, one launch (start us, length us, event | category | flops | bytes accessed | tf_op | source)
XLA Modules:
  0.0 120.5 jit_solution(10425930042593909057)
XLA Ops:
  0.6 0.8 copy.14
  1.4 0.6 reshape.16.mark_s
  2.0 67.7 %shard_map.122 = bf16[16,32,512]{2,1,0:T(8,128)(2,1)} custom-call(s32[16]{0:T(128)} %group_s.1, bf16[16,32,512]{2,1,0:T(8,128)(2,1)} %bitcast.3, bf16[512,128]{1,0:T(8,128)(2,1)} %ck.1, bf16[512,128]{1,0:T(8,128)(2,1)} %cv.1, bf16[1024,128]{1,0:T(8,128)(2,1)} %pk.1, bf16[1024,128]{1,0:T(8,128)(2,1)} %pv.1), custom_call_target="tpu_custom_call" | custom-call | flops 4294967296 | bytes 8388608 | tf_op jit(solution)/shard_map/pallas_call | solution.py:328
  69.7 47.2 %shard_map.123 = (bf16[64,8192]{1,0:T(8,128)(2,1)}, f32[1,128]{1,0:T(1,128)}) custom-call(s32[16]{0:T(128)} %len_s.1, s32[64]{0:T(128)} %reshape.16.mark_s, bf16[4,2,64,512]{3,2,1,0:T(8,128)(2,1)} %bitcast.5, bf16[512,8192]{1,0:T(8,128)(2,1)} %weight.1, bf16[64,8192]{1,0:T(8,128)(2,1)} %residual.1, f32[1,8192]{1,0:T(1,128)} %bitcast.4), custom_call_target="tpu_custom_call" | custom-call | flops 4294967296 | bytes 12582912 | tf_op jit(solution)/shard_map/pallas_call | solution.py:502
  116.9 0.7 slice_reduce_fusion
  117.6 0.6 reshape_squeeze.3
  118.2 2.3 %copy.16 = bf16[64,8192]{1,0:T(8,128)(2,1)} copy(bf16[64,8192]{1,0:T(8,128)(2,1)} %get-tuple-element.8) | data formatting | bytes 2097152

commit v2 on v1

v2 whole, which is shorter than its diff:
```python
import functools
import math

import jax
import jax.numpy as jnp
from jax import lax
from jax.experimental import pallas as pl
from jax.experimental.pallas import tpu as pltpu
from jax.sharding import PartitionSpec as P

HD = 128
P_SIZE = 1024
L = 32
C = 16
PAIR = 2
R = 4
XN, ZN, YN = 4, 8, 4
D = 8192
SCALE = 1.0 / math.sqrt(HD)
LOG2E = 1.4426950408889634
TILE = 512
TILES = D // 2 // TILE
ROWS = C * L // (2 * YN)
F32 = jnp.float32
BF16 = jnp.bfloat16
VMEM_LIMIT = 56 * 1024 * 1024


def remote(src, dst, send_sem, recv_sem, device):
    return pltpu.make_async_remote_copy(
        src_ref=src,
        dst_ref=dst,
        send_sem=send_sem,
        recv_sem=recv_sem,
        device_id=device,
        device_id_type=pl.DeviceIdType.MESH,
    )


def rows_of(block):
    return jnp.concatenate([block[:, r * HD : (r + 1) * HD] for r in range(R)], axis=0)


def with_ones(values):
    return jnp.concatenate([values, jnp.ones(values.shape, values.dtype)], axis=1)


def soften(scores, value_rows):
    highest = jnp.max(scores, axis=-1, keepdims=True)
    raised = jnp.exp2((scores - highest) * (SCALE * LOG2E)).astype(BF16)
    mixed = jnp.dot(raised, with_ones(value_rows), preferred_element_type=F32)
    summed = mixed[:, HD:]
    return mixed[:, :HD] / summed, highest * SCALE + jnp.log(summed)


def scores_of(queries, keys):
    return lax.dot_general(
        queries, keys, (((1,), (1,)), ((), ())), preferred_element_type=F32
    )


def fused_kernel(
    group_s, len_s, mark_s, q_in, ck_in, cv_in, pk, pv, residual_in, weight, head_in,
    hidden, rewards,
    qbuf, ck, cv, kbuf, vbuf, tabv, tabs, res, lsb, rel_r, rel_l, sfo, sfl, slot_s, scores,
    attn, attn_sib, wbuf, part, mine, far_r, far_l, near_l, near_r, residual, head_w, squares, dots,
    loc_sem, tab_ss, tab_rs, q_ss, q_rs, k_ss, k_rs, v_ss, v_rs,
    ret_ss, ret_rs, fwd_ss, fwd_rs, lse_ss, lse_rs,
    w_sem, ws_ss, ws_rs, att_ss, att_rs, far_ss, far_rs, sib_ss, sib_rs,
    now_ss, late_ss, nl_rs, nr_rs,
):
    dp = lax.axis_index("dp")
    x, z = dp // ZN, dp % ZN
    t = lax.axis_index("tensor")
    y, core = t // 2, t % 2

    def at(dp_at, t_at):
        return {"dp": dp_at, "tensor": t_at}

    xl = at(((x + XN - 1) % XN) * ZN + z, t)
    xr = at(((x + 1) % XN) * ZN + z, t)
    xx = at(((x + 2) % XN) * ZN + z, t)
    zl = at(x * ZN + (z + ZN - 1) % ZN, t)
    zr = at(x * ZN + (z + 1) % ZN, t)
    yr_at, yl_at, far_at = (y + 1) % YN, (y + YN - 1) % YN, (y + 2) % YN
    yr = [at(dp, yr_at * 2 + k) for k in range(2)]
    yl = [at(dp, yl_at * 2 + k) for k in range(2)]
    yr_same, yl_same = at(dp, yr_at * 2 + core), at(dp, yl_at * 2 + core)
    sibling = at(dp, y * 2 + 1 - core)

    barrier = pltpu.get_barrier_semaphore()
    peers = [zl, zr, xl, xr, xx, sibling] + yr + yl
    for device in peers:
        pl.semaphore_signal(
            barrier, inc=1, device_id=device, device_id_type=pl.DeviceIdType.MESH
        )

    own_k = pltpu.make_async_copy(pk, kbuf.at[0], loc_sem.at[0])
    own_v = pltpu.make_async_copy(pv, vbuf.at[0], loc_sem.at[1])
    own_q = pltpu.make_async_copy(q_in, qbuf.at[pl.ds(0, C)], loc_sem.at[2])
    own_ck = pltpu.make_async_copy(ck_in, ck, loc_sem.at[4])
    own_cv = pltpu.make_async_copy(cv_in, cv, loc_sem.at[5])
    for copy in (own_q, own_ck, own_cv, own_k, own_v):
        copy.start()

    groups = [group_s[c] for c in range(C)]
    lane = lax.broadcasted_iota(jnp.int32, (8, 128), 1)
    table = jnp.zeros((8, 128), jnp.int32)
    for c in range(C):
        slot = jnp.int32(0)
        for e in range(c):
            slot = slot + jnp.where(groups[e] == groups[c], 1, 0)
        slot = jnp.minimum(slot, PAIR - 1)
        table = jnp.where(lane == groups[c] * PAIR + slot, c, table)
        away = (groups[c] // ZN - x + XN) % XN
        region = jnp.where(away == 0, 0, jnp.where(away == 3, 4, jnp.where(away == 1, 5, 6)))
        back = (z - groups[c] % ZN + ZN) % ZN
        order = jnp.where(back == 0, 0, jnp.where(back <= 4, 2 * back - 1, 2 * (ZN - back)))
        slot_s[c] = region * C + order * PAIR + slot
    tabv[0] = table

    pl.semaphore_wait(barrier, len(peers))

    def k_to(n, src, device):
        return remote(src, kbuf.at[n], k_ss.at[n], k_rs.at[n], device)

    def v_to(n, src, device):
        return remote(src, vbuf.at[n], v_ss.at[n], v_rs.at[n], device)

    k_to(1, pk, zr).start()
    k_to(2, pk, zl).start()
    half = C // 2
    lo, hi = pl.ds(0, half), pl.ds(half, half)

    def q_copy(i, src, region, half_at, device):
        return remote(
            src, qbuf.at[pl.ds(region * C + half_at * half, half)], q_ss.at[i], q_rs.at[i], device
        )

    q_copies = [
        q_copy(0, q_in.at[lo], 1, 0, xr),
        q_copy(1, q_in.at[hi], 2, 1, xl),
        q_copy(2, q_in.at[hi], 1, 1, xr),
        q_copy(3, q_in.at[lo], 2, 0, xl),
        q_copy(4, qbuf.at[pl.ds(1 * C, half)], 3, 0, xr),
        q_copy(5, qbuf.at[pl.ds(2 * C + half, half)], 3, 1, xl),
    ]
    q_copies[0].start()
    q_copies[1].start()
    v_to(1, pv, zr).start()
    v_to(2, pv, zl).start()
    tab_copies = [
        remote(tabv.at[0], tabv.at[1], tab_ss.at[0], tab_rs.at[0], xr),
        remote(tabv.at[0], tabv.at[2], tab_ss.at[1], tab_rs.at[1], xl),
        remote(tabv.at[0], tabv.at[3], tab_ss.at[2], tab_rs.at[2], xx),
    ]
    for copy in tab_copies:
        copy.start()
    q_copies[2].start()
    q_copies[3].start()

    def w_columns(side, i):
        return weight.at[:, pl.ds(pl.multiple_of(side * (D // 2) + i * TILE, TILE), TILE)]

    def w_copy(i):
        return pltpu.make_async_copy(w_columns(core, i), wbuf.at[0, i], w_sem.at[i])

    def w_send(i):
        return remote(w_columns(1 - core, i), wbuf.at[1, i], ws_ss.at[i], ws_rs.at[i], sibling)

    def w_start(i, carry):
        w_copy(i).start()
        w_send(i).start()
        return carry

    lax.fori_loop(0, TILES, w_start, 0)
    res_copy = pltpu.make_async_copy(residual_in, residual, loc_sem.at[6])
    head_copy = pltpu.make_async_copy(head_in, head_w, loc_sem.at[7])
    res_copy.start()
    head_copy.start()

    own_q.wait()
    own_ck.wait()
    own_cv.wait()
    row = lax.broadcasted_iota(jnp.int32, (4 * R * L, 4 * L), 0)
    col = lax.broadcasted_iota(jnp.int32, (4 * R * L, 4 * L), 1)
    allowed = (row // (R * L) == col // L) & (col % L <= row % L)

    def suffix(g, carry):
        queries = jnp.concatenate([rows_of(qbuf[g * 4 + k]) for k in range(4)], axis=0)
        keys = ck[pl.ds(g * 4 * L, 4 * L), :]
        own_scores = jnp.where(allowed, scores_of(queries, keys), -1e30)
        mixed, lse = soften(own_scores, cv[pl.ds(g * 4 * L, 4 * L), :])
        for k in range(4):
            sfo[g * 4 + k] = mixed[k * R * L : (k + 1) * R * L]
            sfl[g * 4 + k] = lse[k * R * L : (k + 1) * R * L]
        return carry

    lax.fori_loop(0, C // 4, suffix, 0)

    q_copies[0].wait_recv()
    q_copies[4].start()
    q_copies[1].wait_recv()
    q_copies[5].start()
    own_k.wait()
    own_v.wait()
    for n, device in ((1, zr), (2, zl)):
        k_to(n, kbuf.at[n], device).wait_recv()
        k_to(n + 2, kbuf.at[n], device).start()
    for n, device in ((1, zr), (2, zl)):
        v_to(n, vbuf.at[n], device).wait_recv()
        v_to(n + 2, vbuf.at[n], device).start()
    for copy in tab_copies:
        copy.wait_recv()
    to_smem = pltpu.make_async_copy(tabv, tabs, loc_sem.at[3])
    to_smem.start()
    for i in (2, 3, 4, 5):
        q_copies[i].wait_recv()
    to_smem.wait()

    eye = lax.broadcasted_iota(jnp.int32, (HD, HD), 0) == lax.broadcasted_iota(
        jnp.int32, (HD, HD), 1
    )

    def pair_at(region, n):
        return pl.ds(region * C + n * PAIR, PAIR)

    def one_at(region, n, u):
        return pl.ds(region * C + n * PAIR + u, 1)

    def returns(n):
        return (
            remote(res.at[pair_at(1, n)], res.at[pair_at(5, n)], ret_ss.at[0, n], ret_rs.at[0, n], xl),
            remote(res.at[pair_at(2, n)], res.at[pair_at(4, n)], ret_ss.at[1, n], ret_rs.at[1, n], xr),
            remote(res.at[one_at(3, n, 0)], rel_r.at[pl.ds(n, 1)], ret_ss.at[2, n], ret_rs.at[2, n], xr),
            remote(res.at[one_at(3, n, 1)], rel_l.at[pl.ds(n, 1)], ret_ss.at[3, n], ret_rs.at[3, n], xl),
        )

    def relays(n):
        return (
            remote(rel_r.at[pl.ds(n, 1)], res.at[one_at(6, n, 0)], fwd_ss.at[0, n], fwd_rs.at[0, n], xr),
            remote(rel_l.at[pl.ds(n, 1)], res.at[one_at(6, n, 1)], fwd_ss.at[1, n], fwd_rs.at[1, n], xl),
        )

    def relay(n):
        _, _, right, left = returns(n)
        on_right, on_left = relays(n)
        right.wait_recv()
        on_right.start()
        left.wait_recv()
        on_left.start()

    def step(n, carry):
        @pl.when(n == 2)
        def _():
            for m, device in ((3, zr), (4, zl)):
                k_to(m, kbuf.at[m], device).wait_recv()
                k_to(m + 2, kbuf.at[m], device).start()

        @pl.when(n == 3)
        def _():
            for m, device in ((3, zr), (4, zl)):
                v_to(m, vbuf.at[m], device).wait_recv()
                v_to(m + 2, vbuf.at[m], device).start()

        @pl.when(n == 5)
        def _():
            k_to(5, kbuf.at[5], zr).wait_recv()
            k_to(7, kbuf.at[5], zr).start()
            k_to(6, kbuf.at[6], zl).wait_recv()
            v_to(6, vbuf.at[6], zl).wait_recv()
            v_to(7, vbuf.at[6], zl).start()
            v_to(5, vbuf.at[5], zr).wait_recv()

        @pl.when(n == 7)
        def _():
            k_to(7, kbuf.at[5], zr).wait_recv()
            v_to(7, vbuf.at[6], zl).wait_recv()

        owner_z = (z + (1 - 2 * (n % 2)) * ((n + 1) // 2) + ZN) % ZN
        base = (x * ZN + owner_z) * PAIR

        def queries_of(s):
            return jnp.concatenate(
                [rows_of(qbuf[s * C + tabs[s, 0, base + u]]) for u in range(PAIR)], axis=0
            )

        scores[0] = scores_of(queries_of(0), kbuf[n])
        for s in range(XN):
            if s + 1 < XN:
                scores[(s + 1) % 2] = scores_of(queries_of(s + 1), kbuf[n])
            mixed, lse = soften(scores[s % 2], vbuf[n])
            mixed = mixed.astype(BF16)
            for u in range(PAIR):
                here = s * C + n * PAIR + u
                for r in range(R):
                    first = (u * R + r) * L
                    res[here, :, r * HD : (r + 1) * HD] = mixed[first : first + L]
                lsb[here] = jnp.sum(
                    jnp.where(eye, lse[u * HD : (u + 1) * HD], 0.0), axis=0, keepdims=True
                )
        for copy in returns(n):
            copy.start()

        @pl.when(n >= 2)
        def _():
            relay(n - 2)

        return carry

    lax.fori_loop(0, ZN, step, 0)
    lse_copies = [
        remote(lsb.at[pl.ds(1 * C, C)], lsb.at[pl.ds(5 * C, C)], lse_ss.at[0], lse_rs.at[0], xl),
        remote(lsb.at[pl.ds(2 * C, C)], lsb.at[pl.ds(4 * C, C)], lse_ss.at[1], lse_rs.at[1], xr),
        remote(lsb.at[pl.ds(3 * C, C)], lsb.at[pl.ds(6 * C, C)], lse_ss.at[2], lse_rs.at[2], xx),
    ]
    for copy in lse_copies:
        copy.start()
    relay(ZN - 2)
    relay(ZN - 1)

    def arrived(n, carry):
        from_xl, from_xr, _, _ = returns(n)
        from_xl.wait_recv()
        from_xr.wait_recv()
        for copy in relays(n):
            copy.wait_recv()
        return carry

    lax.fori_loop(0, ZN, arrived, 0)
    for copy in lse_copies:
        copy.wait_recv()

    def attn_copy(g):
        quarter = pl.ds(g * 4, 4)
        return remote(attn.at[quarter], attn_sib.at[quarter], att_ss.at[g], att_rs.at[g], sibling)

    def merge(g, carry):
        for k in range(4):
            c = g * 4 + k
            where = slot_s[c]
            prefix = rows_of(res[where]).astype(F32)
            prefix_lse = jnp.sum(jnp.where(eye, lsb[where], 0.0), axis=1, keepdims=True)
            suffix_lse = sfl[c]
            largest = jnp.maximum(prefix_lse, suffix_lse)
            a = jnp.exp(prefix_lse - largest)
            b = jnp.exp(suffix_lse - largest)
            joined = ((a * prefix + b * sfo[c]) / (a + b)).astype(BF16)
            for r in range(R):
                attn[c, :, r * HD : (r + 1) * HD] = joined[r * L : (r + 1) * L]
        attn_copy(g).start()
        return carry

    lax.fori_loop(0, C // 4, merge, 0)

    squares[...] = jnp.zeros_like(squares)
    dots[...] = jnp.zeros_like(dots)

    def far_copies(i):
        return (
            remote(part.at[i, far_at, 0], far_r.at[i], far_ss.at[0, i], far_rs.at[0, i], yr_same),
            remote(part.at[i, far_at, 1], far_l.at[i], far_ss.at[1, i], far_rs.at[1, i], yl_same),
        )

    def now_copies(i):
        return (
            remote(part.at[i, yr_at, 1], near_l.at[core, i], now_ss.at[0, i], nl_rs.at[core, i], yr[1]),
            remote(part.at[i, yl_at, 0], near_r.at[core, i], now_ss.at[1, i], nr_rs.at[core, i], yl[0]),
        )

    def late_copies(i):
        return (
            remote(part.at[i, yr_at, 0], near_l.at[core, i], late_ss.at[0, i], nl_rs.at[core, i], yr[0]),
            remote(part.at[i, yl_at, 1], near_r.at[core, i], late_ss.at[1, i], nr_rs.at[core, i], yl[1]),
        )

    def sib_copy(i):
        return remote(part.at[i, y, 1 - core], mine.at[i], sib_ss.at[i], sib_rs.at[i], sibling)

    def near_copies(i, side):
        return (
            remote(near_l.at[side, i], near_l.at[side, i], now_ss.at[0, i], nl_rs.at[side, i], yr[1]),
            remote(near_r.at[side, i], near_r.at[side, i], now_ss.at[1, i], nr_rs.at[side, i], yl[0]),
        )

    def multiply(i):
        w_copy(i).wait()
        w_send(i).wait_recv()
        summed = jnp.dot(
            attn[...].reshape(C * L, R * HD), wbuf[0, i], preferred_element_type=F32
        ) + jnp.dot(
            attn_sib[...].reshape(C * L, R * HD), wbuf[1, i], preferred_element_type=F32
        )
        part[i] = summed.astype(BF16).reshape(YN, 2, ROWS, TILE)
        for copy in far_copies(i) + now_copies(i) + (sib_copy(i),):
            copy.start()

    def pass_on(i):
        to_r, to_l = far_copies(i)
        late_r, late_l = late_copies(i)
        to_r.wait_recv()
        part[i, yr_at, 0] = (part[i, yr_at, 0].astype(F32) + far_r[i].astype(F32)).astype(BF16)
        late_r.start()
        to_l.wait_recv()
        part[i, yl_at, 1] = (part[i, yl_at, 1].astype(F32) + far_l[i].astype(F32)).astype(BF16)
        late_l.start()

    token = lax.broadcasted_iota(jnp.int32, (ROWS, 1), 0)
    first_cand = t * 2
    live = (token % L) < jnp.where(token < L, len_s[first_cand], len_s[first_cand + 1])

    def finish(i):
        sib_copy(i).wait_recv()
        for side in range(2):
            for copy in near_copies(i, side):
                copy.wait_recv()
        for side, kept in ((core, part[i, y, core]), (1 - core, mine[i])):
            columns = pl.ds(pl.multiple_of(side * (D // 2) + i * TILE, TILE), TILE)
            total = (
                residual[:, columns].astype(F32)
                + kept.astype(F32)
                + near_l[side, i].astype(F32)
                + near_r[side, i].astype(F32)
            )
            out = jnp.where(live, total, 0.0).astype(BF16)
            hidden[:, columns] = out
            v = out.astype(F32)
            sq = v * v
            pr = v * head_w[:, columns]
            squares[...] += functools.reduce(
                jnp.add, [sq[:, k * 128 : (k + 1) * 128] for k in range(TILE // 128)]
            )
            dots[...] += functools.reduce(
                jnp.add, [pr[:, k * 128 : (k + 1) * 128] for k in range(TILE // 128)]
            )

    for g in range(C // 4):
        attn_copy(g).wait_recv()
    res_copy.wait()
    head_copy.wait()

    def tile_step(i, carry):
        @pl.when(i < TILES)
        def _():
            multiply(i)

        @pl.when((i >= 1) & (i < TILES + 1))
        def _():
            pass_on(i - 1)

        @pl.when(i >= 2)
        def _():
            finish(i - 2)

        return carry

    lax.fori_loop(0, TILES + 2, tile_step, 0)

    mean = jnp.sum(squares[...], axis=1, keepdims=True) * (1.0 / D)
    logit = jnp.sum(dots[...], axis=1, keepdims=True) * lax.rsqrt(mean + 1e-06)
    reward = 1.0 / (1.0 + jnp.exp(-logit))
    lane_row = lax.broadcasted_iota(jnp.int32, (1, 128), 1)
    for a in range(2):
        wanted = jnp.full((1, 128), -1, jnp.int32)
        for k in range(4):
            wanted = jnp.where(lane_row == k, a * L + mark_s[k, first_cand + a], wanted)
        picked = jnp.sum(jnp.where(token == wanted, reward, 0.0), axis=0, keepdims=True)
        rewards[a : a + 1, :] = picked[:, :4]

    def sent(n, carry):
        for copy in returns(n) + relays(n):
            copy.wait_send()
        return carry

    lax.fori_loop(0, ZN, sent, 0)
    for copy in lse_copies + q_copies + tab_copies:
        copy.wait_send()
    for n in range(1, ZN):
        k_to(n, kbuf.at[0], zr).wait_send()
        v_to(n, vbuf.at[0], zr).wait_send()
    for g in range(C // 4):
        attn_copy(g).wait_send()

    def tile_sent(i, carry):
        w_send(i).wait_send()
        sib_copy(i).wait_send()
        for copy in far_copies(i) + now_copies(i) + late_copies(i):
            copy.wait_send()
        return carry

    lax.fori_loop(0, TILES, tile_sent, 0)


def fused(group, lens, marks, q, ck, cv, pk, pv, residual, weight, head_w):
    dma = pltpu.SemaphoreType.DMA
    any_space = pl.BlockSpec(memory_space=pl.ANY)
    vmem = pl.BlockSpec(memory_space=pltpu.VMEM)
    smem = pl.BlockSpec(memory_space=pltpu.SMEM)
    return pl.pallas_call(
        fused_kernel,
        out_shape=(
            jax.ShapeDtypeStruct((ROWS, D), BF16),
            jax.ShapeDtypeStruct((2, 4), F32),
        ),
        in_specs=[smem] * 3 + [any_space] * 8,
        out_specs=(vmem, vmem),
        scratch_shapes=[
            pltpu.VMEM((XN * C, L, R * HD), BF16),
            pltpu.VMEM((C * L, HD), BF16),
            pltpu.VMEM((C * L, HD), BF16),
            pltpu.VMEM((ZN, P_SIZE, HD), BF16),
            pltpu.VMEM((ZN, P_SIZE, HD), BF16),
            pltpu.VMEM((XN, 8, 128), jnp.int32),
            pltpu.SMEM((XN, 8, 128), jnp.int32),
            pltpu.VMEM((7 * C, L, R * HD), BF16),
            pltpu.VMEM((7 * C, 1, HD), F32),
            pltpu.VMEM((ZN, L, R * HD), BF16),
            pltpu.VMEM((ZN, L, R * HD), BF16),
            pltpu.VMEM((C, R * L, HD), F32),
            pltpu.VMEM((C, R * L, HD), F32),
            pltpu.SMEM((C,), jnp.int32),
            pltpu.VMEM((2, PAIR * R * L, P_SIZE), F32),
            pltpu.VMEM((C, L, R * HD), BF16),
            pltpu.VMEM((C, L, R * HD), BF16),
            pltpu.VMEM((2, TILES, R * HD, TILE), BF16),
            pltpu.VMEM((TILES, YN, 2, ROWS, TILE), BF16),
            pltpu.VMEM((TILES, ROWS, TILE), BF16),
            pltpu.VMEM((TILES, ROWS, TILE), BF16),
            pltpu.VMEM((TILES, ROWS, TILE), BF16),
            pltpu.VMEM((2, TILES, ROWS, TILE), BF16),
            pltpu.VMEM((2, TILES, ROWS, TILE), BF16),
            pltpu.VMEM((ROWS, D), BF16),
            pltpu.VMEM((1, D), F32),
            pltpu.VMEM((ROWS, 128), F32),
            pltpu.VMEM((ROWS, 128), F32),
            dma((8,)), dma((3,)), dma((3,)), dma((6,)), dma((6,)),
            dma((ZN,)), dma((ZN,)), dma((ZN,)), dma((ZN,)),
            dma((4, ZN)), dma((4, ZN)), dma((2, ZN)), dma((2, ZN)), dma((3,)), dma((3,)),
            dma((TILES,)), dma((TILES,)), dma((TILES,)), dma((4,)), dma((4,)),
            dma((2, TILES)), dma((2, TILES)), dma((TILES,)), dma((TILES,)),
            dma((2, TILES)), dma((2, TILES)), dma((2, TILES)), dma((2, TILES)),
        ],
        compiler_params=pltpu.CompilerParams(
            collective_id=0, has_side_effects=True, vmem_limit_bytes=VMEM_LIMIT
        ),
        cost_estimate=pl.CostEstimate(
            flops=2 * 2 * 64 * 128 * P_SIZE * HD + 2 * C * L * R * HD * D,
            bytes_accessed=16 << 20,
            transcendentals=8 << 20,
        ),
    )(group, lens, marks, q, ck, cv, pk, pv, residual, weight, head_w)


def local(
    cand_q, cand_k, cand_v, prompt_k, prompt_v, cand_group, cand_len, boundaries,
    residual, out_weight, head_weight,
):
    hidden, rewards = fused(
        cand_group,
        cand_len,
        boundaries.T,
        cand_q.reshape(C, L, R * HD),
        cand_k,
        cand_v,
        prompt_k,
        prompt_v,
        residual,
        out_weight,
        head_weight.reshape(1, D),
    )
    return hidden, rewards


def solution(mesh):
    in_specs = (
        P("dp", "tensor"),
        P("dp", "tensor"),
        P("dp", "tensor"),
        P("dp", "tensor"),
        P("dp", "tensor"),
        P("dp"),
        P("dp"),
        P("dp", None),
        P(("dp", "tensor"), None),
        P("tensor", None),
        P(),
    )
    out_specs = (P(("dp", "tensor"), None), P(("dp", "tensor"), None))
    return jax.shard_map(local, mesh=mesh, in_specs=in_specs, out_specs=out_specs, check_vma=False)
```

time: 121 us -> 108 us (0.89)
  Pallas kernels: 115 us -> 103 us
  local copies, waits for them, and re-layouts: 4.92 us -> 3.5 us
    pallas_call x2 -> x1, Pallas kernels: 115 us -> 103 us  [fused(): pl.pallas_call(fused_kernel, out_shape=(jax.ShapeDtypeStruct((ROWS, D), B...]
where the time goes in v2:
time: 108 us
  Pallas kernels  103 us (95%)
  local copies, waits for them, and re-layouts  3.5 us (3%)
    pallas_call x1, Pallas kernels, fused(): pl.pallas_call(fused_kernel, out_shape=(jax.ShapeDtypeStruct((ROWS, D), B...  103 us
    unnamed x2, local copies, waits for them, and re-layouts  3.5 us

profile of v2, /device:TPU:1, one launch (start us, length us, event | category | flops | bytes accessed | tf_op | source)
XLA Modules:
  0.0 107.5 jit_solution(7560773154562347670)
XLA Ops:
  0.6 103.4 %shard_map.122 = (bf16[64,8192]{1,0:T(8,128)(2,1)}, f32[2,4]{1,0:T(2,128)}) custom-call(s32[16]{0:T(128)} %group_s.1, s32[16]{0:T(128)} %len_s.1, s32[4,16]{1,0:T(4,128)} %bitcast.5, bf16[16,32,512]{2,1,0:T(8,128)(2,1)} %bitcast.3, bf16[512,128]{1,0:T(8,128)(2,1)} %ck_in.1, bf16[512,128]{1,0:T(8,128)(2,1)} %cv_in.1, bf16[1024,128]{1,0:T(8,128)(2,1)} %pk.1, ...), custom_call_target="tpu_custom_call" | custom-call | flops 8589934592 | bytes 16777216 | tf_op jit(solution)/shard_map/pallas_call | solution.py:499
  104.0 2.3 %copy.15 = bf16[64,8192]{1,0:T(8,128)(2,1)} copy(bf16[64,8192]{1,0:T(8,128)(2,1)} %get-tuple-element.4) | data formatting | bytes 2097152
  106.3 1.2 %copy.16 = f32[2,4]{1,0:T(2,128)} copy(f32[2,4]{1,0:T(2,128)} %get-tuple-element.5) | data formatting | bytes 64

commit v3 on v2

--- a/solution.py
+++ b/solution.py
@@ -20,6 +20,7 @@
 LOG2E = 1.4426950408889634
 TILE = 512
 TILES = D // 2 // TILE
+AHEAD, BEHIND = 2, 4
 ROWS = C * L // (2 * YN)
 F32 = jnp.float32
 BF16 = jnp.bfloat16
@@ -63,11 +64,10 @@
     group_s, len_s, mark_s, q_in, ck_in, cv_in, pk, pv, residual_in, weight, head_in,
     hidden, rewards,
     qbuf, ck, cv, kbuf, vbuf, tabv, tabs, res, lsb, rel_r, rel_l, sfo, sfl, slot_s, scores,
-    attn, attn_sib, wbuf, part, mine, far_r, far_l, near_l, near_r, residual, head_w, squares, dots,
+    attn, attn_sib, wbuf, part, far, near, residual, head_w, squares, dots,
     loc_sem, tab_ss, tab_rs, q_ss, q_rs, k_ss, k_rs, v_ss, v_rs,
-    ret_ss, ret_rs, fwd_ss, fwd_rs, lse_ss, lse_rs,
-    w_sem, ws_ss, ws_rs, att_ss, att_rs, far_ss, far_rs, sib_ss, sib_rs,
-    now_ss, late_ss, nl_rs, nr_rs,
+    ret_ss, ret_rs, rel_rs, fwd_ss, lse_ss, lse_rs,
+    w_sem, ws_ss, ws_rs, att_ss, att_rs, far_ss, far_rs, sib_ss, now_ss, late_ss, near_rs,
 ):
     dp = lax.axis_index("dp")
     x, z = dp // ZN, dp % ZN
@@ -95,6 +95,38 @@
             barrier, inc=1, device_id=device, device_id_type=pl.DeviceIdType.MESH
         )
 
+    pl.semaphore_wait(barrier, len(peers))
+
+    def k_to(n, src, device):
+        return remote(src, kbuf.at[n], k_ss, k_rs.at[n], device)
+
+    def v_to(n, src, device):
+        return remote(src, vbuf.at[n], v_ss, v_rs.at[n], device)
+
+    k_to(1, pk, zr).start()
+    k_to(2, pk, zl).start()
+    half = C // 2
+    lo, hi = pl.ds(0, half), pl.ds(half, half)
+
+    def q_copy(i, src, region, half_at, device):
+        return remote(
+            src, qbuf.at[pl.ds(region * C + half_at * half, half)], q_ss, q_rs.at[min(i, 2)], device
+        )
+
+    q_copies = [
+        q_copy(0, q_in.at[lo], 1, 0, xr),
+        q_copy(1, q_in.at[hi], 2, 1, xl),
+        q_copy(2, q_in.at[hi], 1, 1, xr),
+        q_copy(3, q_in.at[lo], 2, 0, xl),
+        q_copy(4, qbuf.at[pl.ds(1 * C, half)], 3, 0, xr),
+        q_copy(5, qbuf.at[pl.ds(2 * C + half, half)], 3, 1, xl),
+    ]
+    q_copies[0].start()
+    q_copies[1].start()
+    v_to(1, pv, zr).start()
+    v_to(2, pv, zl).start()
+    q_copies[2].start()
+    q_copies[3].start()
     own_k = pltpu.make_async_copy(pk, kbuf.at[0], loc_sem.at[0])
     own_v = pltpu.make_async_copy(pv, vbuf.at[0], loc_sem.at[1])
     own_q = pltpu.make_async_copy(q_in, qbuf.at[pl.ds(0, C)], loc_sem.at[2])
@@ -102,7 +134,6 @@
     own_cv = pltpu.make_async_copy(cv_in, cv, loc_sem.at[5])
     for copy in (own_q, own_ck, own_cv, own_k, own_v):
         copy.start()
-
     groups = [group_s[c] for c in range(C)]
     lane = lax.broadcasted_iota(jnp.int32, (8, 128), 1)
     table = jnp.zeros((8, 128), jnp.int32)
@@ -118,55 +149,22 @@
         order = jnp.where(back == 0, 0, jnp.where(back <= 4, 2 * back - 1, 2 * (ZN - back)))
         slot_s[c] = region * C + order * PAIR + slot
     tabv[0] = table
-
-    pl.semaphore_wait(barrier, len(peers))
-
-    def k_to(n, src, device):
-        return remote(src, kbuf.at[n], k_ss.at[n], k_rs.at[n], device)
-
-    def v_to(n, src, device):
-        return remote(src, vbuf.at[n], v_ss.at[n], v_rs.at[n], device)
-
-    k_to(1, pk, zr).start()
-    k_to(2, pk, zl).start()
-    half = C // 2
-    lo, hi = pl.ds(0, half), pl.ds(half, half)
-
-    def q_copy(i, src, region, half_at, device):
-        return remote(
-            src, qbuf.at[pl.ds(region * C + half_at * half, half)], q_ss.at[i], q_rs.at[i], device
-        )
-
-    q_copies = [
-        q_copy(0, q_in.at[lo], 1, 0, xr),
-        q_copy(1, q_in.at[hi], 2, 1, xl),
-        q_copy(2, q_in.at[hi], 1, 1, xr),
-        q_copy(3, q_in.at[lo], 2, 0, xl),
-        q_copy(4, qbuf.at[pl.ds(1 * C, half)], 3, 0, xr),
-        q_copy(5, qbuf.at[pl.ds(2 * C + half, half)], 3, 1, xl),
-    ]
-    q_copies[0].start()
-    q_copies[1].start()
-    v_to(1, pv, zr).start()
-    v_to(2, pv, zl).start()
     tab_copies = [
-        remote(tabv.at[0], tabv.at[1], tab_ss.at[0], tab_rs.at[0], xr),
-        remote(tabv.at[0], tabv.at[2], tab_ss.at[1], tab_rs.at[1], xl),
-        remote(tabv.at[0], tabv.at[3], tab_ss.at[2], tab_rs.at[2], xx),
+        remote(tabv.at[0], tabv.at[1], tab_ss, tab_rs, xr),
+        remote(tabv.at[0], tabv.at[2], tab_ss, tab_rs, xl),
+        remote(tabv.at[0], tabv.at[3], tab_ss, tab_rs, xx),
     ]
     for copy in tab_copies:
         copy.start()
-    q_copies[2].start()
-    q_copies[3].start()
 
     def w_columns(side, i):
         return weight.at[:, pl.ds(pl.multiple_of(side * (D // 2) + i * TILE, TILE), TILE)]
 
     def w_copy(i):
-        return pltpu.make_async_copy(w_columns(core, i), wbuf.at[0, i], w_sem.at[i])
+        return pltpu.make_async_copy(w_columns(core, i), wbuf.at[0, i], w_sem)
 
     def w_send(i):
-        return remote(w_columns(1 - core, i), wbuf.at[1, i], ws_ss.at[i], ws_rs.at[i], sibling)
+        return remote(w_columns(1 - core, i), wbuf.at[1, i], ws_ss, ws_rs, sibling)
 
     def w_start(i, carry):
         w_copy(i).start()
@@ -210,12 +208,12 @@
     for n, device in ((1, zr), (2, zl)):
         v_to(n, vbuf.at[n], device).wait_recv()
         v_to(n + 2, vbuf.at[n], device).start()
-    for copy in tab_copies:
-        copy.wait_recv()
+    tab_all = remote(tabv.at[pl.ds(1, 3)], tabv.at[pl.ds(1, 3)], tab_ss, tab_rs, xl)
+    tab_all.wait_recv()
     to_smem = pltpu.make_async_copy(tabv, tabs, loc_sem.at[3])
     to_smem.start()
-    for i in (2, 3, 4, 5):
-        q_copies[i].wait_recv()
+    q_rest = qbuf.at[pl.ds(2 * C, 2 * C)]
+    remote(q_rest, q_rest, q_ss, q_rs.at[2], xl).wait_recv()
     to_smem.wait()
 
     eye = lax.broadcasted_iota(jnp.int32, (HD, HD), 0) == lax.broadcasted_iota(
@@ -230,16 +228,16 @@
 
     def returns(n):
         return (
-            remote(res.at[pair_at(1, n)], res.at[pair_at(5, n)], ret_ss.at[0, n], ret_rs.at[0, n], xl),
-            remote(res.at[pair_at(2, n)], res.at[pair_at(4, n)], ret_ss.at[1, n], ret_rs.at[1, n], xr),
-            remote(res.at[one_at(3, n, 0)], rel_r.at[pl.ds(n, 1)], ret_ss.at[2, n], ret_rs.at[2, n], xr),
-            remote(res.at[one_at(3, n, 1)], rel_l.at[pl.ds(n, 1)], ret_ss.at[3, n], ret_rs.at[3, n], xl),
+            remote(res.at[pair_at(1, n)], res.at[pair_at(5, n)], ret_ss, ret_rs, xl),
+            remote(res.at[pair_at(2, n)], res.at[pair_at(4, n)], ret_ss, ret_rs, xr),
+            remote(res.at[one_at(3, n, 0)], rel_r.at[pl.ds(n, 1)], ret_ss, rel_rs.at[0, n], xr),
+            remote(res.at[one_at(3, n, 1)], rel_l.at[pl.ds(n, 1)], ret_ss, rel_rs.at[1, n], xl),
         )
 
     def relays(n):
         return (
-            remote(rel_r.at[pl.ds(n, 1)], res.at[one_at(6, n, 0)], fwd_ss.at[0, n], fwd_rs.at[0, n], xr),
-            remote(rel_l.at[pl.ds(n, 1)], res.at[one_at(6, n, 1)], fwd_ss.at[1, n], fwd_rs.at[1, n], xl),
+            remote(rel_r.at[pl.ds(n, 1)], res.at[one_at(6, n, 0)], fwd_ss, ret_rs, xr),
+            remote(rel_l.at[pl.ds(n, 1)], res.at[one_at(6, n, 1)], fwd_ss, ret_rs, xl),
         )
 
     def relay(n):
@@ -310,30 +308,24 @@
 
     lax.fori_loop(0, ZN, step, 0)
     lse_copies = [
-        remote(lsb.at[pl.ds(1 * C, C)], lsb.at[pl.ds(5 * C, C)], lse_ss.at[0], lse_rs.at[0], xl),
-        remote(lsb.at[pl.ds(2 * C, C)], lsb.at[pl.ds(4 * C, C)], lse_ss.at[1], lse_rs.at[1], xr),
-        remote(lsb.at[pl.ds(3 * C, C)], lsb.at[pl.ds(6 * C, C)], lse_ss.at[2], lse_rs.at[2], xx),
+        remote(lsb.at[pl.ds(1 * C, C)], lsb.at[pl.ds(5 * C, C)], lse_ss, lse_rs, xl),
+        remote(lsb.at[pl.ds(2 * C, C)], lsb.at[pl.ds(4 * C, C)], lse_ss, lse_rs, xr),
+        remote(lsb.at[pl.ds(3 * C, C)], lsb.at[pl.ds(6 * C, C)], lse_ss, lse_rs, xx),
     ]
     for copy in lse_copies:
         copy.start()
     relay(ZN - 2)
     relay(ZN - 1)
 
-    def arrived(n, carry):
-        from_xl, from_xr, _, _ = returns(n)
-        from_xl.wait_recv()
-        from_xr.wait_recv()
-        for copy in relays(n):
-            copy.wait_recv()
-        return carry
-
-    lax.fori_loop(0, ZN, arrived, 0)
-    for copy in lse_copies:
-        copy.wait_recv()
+    came = pl.ds(4 * C, 3 * C)
+    res_all = remote(res.at[came], res.at[came], fwd_ss, ret_rs, xl)
+    lse_all = remote(lsb.at[came], lsb.at[came], lse_ss, lse_rs, xl)
+    res_all.wait_recv()
+    lse_all.wait_recv()
 
     def attn_copy(g):
         quarter = pl.ds(g * 4, 4)
-        return remote(attn.at[quarter], attn_sib.at[quarter], att_ss.at[g], att_rs.at[g], sibling)
+        return remote(attn.at[quarter], attn_sib.at[quarter], att_ss, att_rs, sibling)
 
     def merge(g, carry):
         for k in range(4):
@@ -358,34 +350,26 @@
 
     def far_copies(i):
         return (
-            remote(part.at[i, far_at, 0], far_r.at[i], far_ss.at[0, i], far_rs.at[0, i], yr_same),
-            remote(part.at[i, far_at, 1], far_l.at[i], far_ss.at[1, i], far_rs.at[1, i], yl_same),
+            remote(part.at[i, far_at, 0], far.at[i, 0], far_ss, far_rs.at[i], yr_same),
+            remote(part.at[i, far_at, 1], far.at[i, 1], far_ss, far_rs.at[i], yl_same),
         )
 
     def now_copies(i):
         return (
-            remote(part.at[i, yr_at, 1], near_l.at[core, i], now_ss.at[0, i], nl_rs.at[core, i], yr[1]),
-            remote(part.at[i, yl_at, 0], near_r.at[core, i], now_ss.at[1, i], nr_rs.at[core, i], yl[0]),
+            remote(part.at[i, yr_at, 1], near.at[i, core], now_ss, near_rs.at[i], yr[1]),
+            remote(part.at[i, yl_at, 0], near.at[i, 2 + core], now_ss, near_rs.at[i], yl[0]),
         )
 
     def late_copies(i):
         return (
-            remote(part.at[i, yr_at, 0], near_l.at[core, i], late_ss.at[0, i], nl_rs.at[core, i], yr[0]),
-            remote(part.at[i, yl_at, 1], near_r.at[core, i], late_ss.at[1, i], nr_rs.at[core, i], yl[1]),
+            remote(part.at[i, yr_at, 0], near.at[i, core], late_ss, near_rs.at[i], yr[0]),
+            remote(part.at[i, yl_at, 1], near.at[i, 2 + core], late_ss, near_rs.at[i], yl[1]),
         )
 
     def sib_copy(i):
-        return remote(part.at[i, y, 1 - core], mine.at[i], sib_ss.at[i], sib_rs.at[i], sibling)
-
-    def near_copies(i, side):
-        return (
-            remote(near_l.at[side, i], near_l.at[side, i], now_ss.at[0, i], nl_rs.at[side, i], yr[1]),
-            remote(near_r.at[side, i], near_r.at[side, i], now_ss.at[1, i], nr_rs.at[side, i], yl[0]),
-        )
+        return remote(part.at[i, y, 1 - core], near.at[i, 4], sib_ss, near_rs.at[i], sibling)
 
     def multiply(i):
-        w_copy(i).wait()
-        w_send(i).wait_recv()
         summed = jnp.dot(
             attn[...].reshape(C * L, R * HD), wbuf[0, i], preferred_element_type=F32
         ) + jnp.dot(
@@ -396,13 +380,11 @@
             copy.start()
 
     def pass_on(i):
-        to_r, to_l = far_copies(i)
         late_r, late_l = late_copies(i)
-        to_r.wait_recv()
-        part[i, yr_at, 0] = (part[i, yr_at, 0].astype(F32) + far_r[i].astype(F32)).astype(BF16)
+        remote(far.at[i], far.at[i], far_ss, far_rs.at[i], yr_same).wait_recv()
+        part[i, yr_at, 0] = (part[i, yr_at, 0].astype(F32) + far[i, 0].astype(F32)).astype(BF16)
         late_r.start()
-        to_l.wait_recv()
-        part[i, yl_at, 1] = (part[i, yl_at, 1].astype(F32) + far_l[i].astype(F32)).astype(BF16)
+        part[i, yl_at, 1] = (part[i, yl_at, 1].astype(F32) + far[i, 1].astype(F32)).astype(BF16)
         late_l.start()
 
     token = lax.broadcasted_iota(jnp.int32, (ROWS, 1), 0)
@@ -410,17 +392,14 @@
     live = (token % L) < jnp.where(token < L, len_s[first_cand], len_s[first_cand + 1])
 
     def finish(i):
-        sib_copy(i).wait_recv()
-        for side in range(2):
-            for copy in near_copies(i, side):
-                copy.wait_recv()
-        for side, kept in ((core, part[i, y, core]), (1 - core, mine[i])):
+        remote(near.at[i], near.at[i], now_ss, near_rs.at[i], yr_same).wait_recv()
+        for side, kept in ((core, part[i, y, core]), (1 - core, near[i, 4])):
             columns = pl.ds(pl.multiple_of(side * (D // 2) + i * TILE, TILE), TILE)
             total = (
                 residual[:, columns].astype(F32)
                 + kept.astype(F32)
-                + near_l[side, i].astype(F32)
-                + near_r[side, i].astype(F32)
+                + near[i, side].astype(F32)
+                + near[i, 2 + side].astype(F32)
             )
             out = jnp.where(live, total, 0.0).astype(BF16)
             hidden[:, columns] = out
@@ -434,27 +413,47 @@
                 jnp.add, [pr[:, k * 128 : (k + 1) * 128] for k in range(TILE // 128)]
             )
 
-    for g in range(C // 4):
-        attn_copy(g).wait_recv()
+    pltpu.make_async_copy(wbuf.at[0], wbuf.at[0], w_sem).wait()
+    w_all = remote(wbuf.at[1], wbuf.at[1], ws_ss, ws_rs, sibling)
+    w_all.wait_recv()
+    attn_all = remote(attn, attn_sib, att_ss, att_rs, sibling)
+    attn_all.wait_recv()
     res_copy.wait()
     head_copy.wait()
 
+    def all_sent():
+        others, queries = pl.ds(1, ZN - 1), pl.ds(C, 3 * C)
+        for copy in (
+            remote(kbuf.at[others], kbuf.at[others], k_ss, k_rs.at[0], zr),
+            remote(vbuf.at[others], vbuf.at[others], v_ss, v_rs.at[0], zr),
+            remote(qbuf.at[queries], qbuf.at[queries], q_ss, q_rs.at[0], xr),
+            remote(res.at[queries], res.at[queries], ret_ss, ret_rs, xr),
+            remote(res.at[pl.ds(0, C)], res.at[pl.ds(0, C)], fwd_ss, ret_rs, xr),
+            tab_all, lse_all, w_all, attn_all,
+        ):
+            copy.wait_send()
+
     def tile_step(i, carry):
         @pl.when(i < TILES)
         def _():
             multiply(i)
 
-        @pl.when((i >= 1) & (i < TILES + 1))
-        def _():
-            pass_on(i - 1)
-
-        @pl.when(i >= 2)
-        def _():
-            finish(i - 2)
+        @pl.when((i >= AHEAD) & (i < TILES + AHEAD))
+        def _():
+            pass_on(i - AHEAD)
+
+        @pl.when(i >= BEHIND)
+        def _():
+            finish(i - BEHIND)
 
         return carry
 
-    lax.fori_loop(0, TILES + 2, tile_step, 0)
+    lax.fori_loop(0, TILES + BEHIND, tile_step, 0)
+    all_sent()
+    tiles = near.at[:, pl.ds(0, 2)]
+    for sem in (far_ss, now_ss, late_ss):
+        remote(tiles, tiles, sem, near_rs.at[0], yr_same).wait_send()
+    remote(far.at[:, 0], far.at[:, 0], sib_ss, near_rs.at[0], sibling).wait_send()
 
     mean = jnp.sum(squares[...], axis=1, keepdims=True) * (1.0 / D)
     logit = jnp.sum(dots[...], axis=1, keepdims=True) * lax.rsqrt(mean + 1e-06)
@@ -467,29 +466,6 @@
         picked = jnp.sum(jnp.where(token == wanted, reward, 0.0), axis=0, keepdims=True)
         rewards[a : a + 1, :] = picked[:, :4]
 
-    def sent(n, carry):
-        for copy in returns(n) + relays(n):
-            copy.wait_send()
-        return carry
-
-    lax.fori_loop(0, ZN, sent, 0)
-    for copy in lse_copies + q_copies + tab_copies:
-        copy.wait_send()
-    for n in range(1, ZN):
-        k_to(n, kbuf.at[0], zr).wait_send()
-        v_to(n, vbuf.at[0], zr).wait_send()
-    for g in range(C // 4):
-        attn_copy(g).wait_send()
-
-    def tile_sent(i, carry):
-        w_send(i).wait_send()
-        sib_copy(i).wait_send()
-        for copy in far_copies(i) + now_copies(i) + late_copies(i):
-            copy.wait_send()
-        return carry
-
-    lax.fori_loop(0, TILES, tile_sent, 0)
-
 
 def fused(group, lens, marks, q, ck, cv, pk, pv, residual, weight, head_w):
     dma = pltpu.SemaphoreType.DMA
@@ -499,8 +475,8 @@
     return pl.pallas_call(
         fused_kernel,
         out_shape=(
-            jax.ShapeDtypeStruct((ROWS, D), BF16),
-            jax.ShapeDtypeStruct((2, 4), F32),
+            pltpu.VMEM((ROWS, D), BF16),
+            pltpu.VMEM((2, 4), F32),
         ),
         in_specs=[smem] * 3 + [any_space] * 8,
         out_specs=(vmem, vmem),
@@ -524,21 +500,15 @@
             pltpu.VMEM((C, L, R * HD), BF16),
             pltpu.VMEM((2, TILES, R * HD, TILE), BF16),
             pltpu.VMEM((TILES, YN, 2, ROWS, TILE), BF16),
-            pltpu.VMEM((TILES, ROWS, TILE), BF16),
-            pltpu.VMEM((TILES, ROWS, TILE), BF16),
-            pltpu.VMEM((TILES, ROWS, TILE), BF16),
-            pltpu.VMEM((2, TILES, ROWS, TILE), BF16),
-            pltpu.VMEM((2, TILES, ROWS, TILE), BF16),
+            pltpu.VMEM((TILES, 2, ROWS, TILE), BF16),
+            pltpu.VMEM((TILES, 5, ROWS, TILE), BF16),
             pltpu.VMEM((ROWS, D), BF16),
             pltpu.VMEM((1, D), F32),
             pltpu.VMEM((ROWS, 128), F32),
             pltpu.VMEM((ROWS, 128), F32),
-            dma((8,)), dma((3,)), dma((3,)), dma((6,)), dma((6,)),
-            dma((ZN,)), dma((ZN,)), dma((ZN,)), dma((ZN,)),
-            dma((4, ZN)), dma((4, ZN)), dma((2, ZN)), dma((2, ZN)), dma((3,)), dma((3,)),
-            dma((TILES,)), dma((TILES,)), dma((TILES,)), dma((4,)), dma((4,)),
-            dma((2, TILES)), dma((2, TILES)), dma((TILES,)), dma((TILES,)),
-            dma((2, TILES)), dma((2, TILES)), dma((2, TILES)), dma((2, TILES)),
+            dma((8,)), dma, dma, dma, dma((3,)), dma, dma((ZN,)), dma, dma((ZN,)),
+            dma, dma, dma((2, ZN)), dma, dma, dma,
+            dma, dma, dma, dma, dma, dma, dma((TILES,)), dma, dma, dma, dma((TILES,)),
         ],
         compiler_params=pltpu.CompilerParams(
             collective_id=0, has_side_effects=True, vmem_limit_bytes=VMEM_LIMIT

time: 108 us -> 102 us (0.944)
  Pallas kernels: 103 us -> 100 us
  local copies, waits for them, and re-layouts: 3.5 us -> 1.53 us
    pallas_call x1, Pallas kernels: 103 us -> 100 us  [fused(): pl.pallas_call(fused_kernel, out_shape=(pltpu.VMEM((ROWS, D), BF16), pltp...]
    unnamed x2, local copies, waits for them, and re-layouts: 3.5 us -> 1.53 us
where the time goes in v3:
time: 102 us
  Pallas kernels  100 us (98%)
  local copies, waits for them, and re-layouts  1.53 us (2%)
    pallas_call x1, Pallas kernels, fused(): pl.pallas_call(fused_kernel, out_shape=(pltpu.VMEM((ROWS, D), BF16), pltp...  100 us

profile of v3, /device:TPU:1, one launch (start us, length us, event | category | flops | bytes accessed | tf_op | source)
XLA Modules:
  0.0 102.3 jit_solution(14622098219927752462)
XLA Ops:
  0.6 100.1 %shard_map.122 = (bf16[64,8192]{1,0:T(8,128)(2,1)S(1)}, f32[2,4]{1,0:T(2,128)S(1)}) custom-call(s32[16]{0:T(128)} %group_s.1, s32[16]{0:T(128)} %len_s.1, s32[4,16]{1,0:T(4,128)} %bitcast.5, bf16[16,32,512]{2,1,0:T(8,128)(2,1)} %bitcast.3, bf16[512,128]{1,0:T(8,128)(2,1)} %ck_in.1, bf16[512,128]{1,0:T(8,128)(2,1)} %cv_in.1, bf16[1024,128]{1,0:T(8,128)(2,1)} %pk.1, ...), custom_call_target="tpu_custom_call" | custom-call | flops 8589934592 | bytes 16777216 | tf_op jit(solution)/shard_map/pallas_call | solution.py:475
  100.7 1.0 copy.15
  101.7 0.6 copy.16

commit v4 on v3

--- a/solution.py
+++ b/solution.py
@@ -63,10 +63,10 @@
 def fused_kernel(
     group_s, len_s, mark_s, q_in, ck_in, cv_in, pk, pv, residual_in, weight, head_in,
     hidden, rewards,
-    qbuf, ck, cv, kbuf, vbuf, tabv, tabs, res, lsb, rel_r, rel_l, sfo, sfl, slot_s, scores,
+    qbuf, qfar, ck, cv, kbuf, vbuf, tabv, tabs, res, lsb, sfo, sfl, slot_s, scores,
     attn, attn_sib, wbuf, part, far, near, residual, head_w, squares, dots,
     loc_sem, tab_ss, tab_rs, q_ss, q_rs, k_ss, k_rs, v_ss, v_rs,
-    ret_ss, ret_rs, rel_rs, fwd_ss, lse_ss, lse_rs,
+    ret_ss, ret_rs, lse_ss, lse_rs,
     w_sem, ws_ss, ws_rs, att_ss, att_rs, far_ss, far_rs, sib_ss, now_ss, late_ss, near_rs,
 ):
     dp = lax.axis_index("dp")
@@ -108,18 +108,19 @@
     half = C // 2
     lo, hi = pl.ds(0, half), pl.ds(half, half)
 
-    def q_copy(i, src, region, half_at, device):
-        return remote(
-            src, qbuf.at[pl.ds(region * C + half_at * half, half)], q_ss, q_rs.at[min(i, 2)], device
-        )
+    def q_copy(sem, src, dst, device):
+        return remote(src, dst, q_ss, q_rs.at[sem], device)
+
+    def q_half(region, half_at):
+        return qbuf.at[pl.ds(region * C + half_at * half, half)]
 
     q_copies = [
-        q_copy(0, q_in.at[lo], 1, 0, xr),
-        q_copy(1, q_in.at[hi], 2, 1, xl),
-        q_copy(2, q_in.at[hi], 1, 1, xr),
-        q_copy(3, q_in.at[lo], 2, 0, xl),
-        q_copy(4, qbuf.at[pl.ds(1 * C, half)], 3, 0, xr),
-        q_copy(5, qbuf.at[pl.ds(2 * C + half, half)], 3, 1, xl),
+        q_copy(0, q_in.at[lo], q_half(1, 0), xr),
+        q_copy(1, q_in.at[hi], q_half(2, 1), xl),
+        q_copy(2, q_in.at[hi], q_half(1, 1), xr),
+        q_copy(2, q_in.at[lo], q_half(2, 0), xl),
+        q_copy(3, q_half(1, 0), qfar.at[lo], xr),
+        q_copy(3, q_half(2, 1), qfar.at[hi], xl),
     ]
     q_copies[0].start()
     q_copies[1].start()
@@ -212,8 +213,7 @@
     tab_all.wait_recv()
     to_smem = pltpu.make_async_copy(tabv, tabs, loc_sem.at[3])
     to_smem.start()
-    q_rest = qbuf.at[pl.ds(2 * C, 2 * C)]
-    remote(q_rest, q_rest, q_ss, q_rs.at[2], xl).wait_recv()
+    remote(qfar, qfar, q_ss, q_rs.at[2], xl).wait_recv()
     to_smem.wait()
 
     eye = lax.broadcasted_iota(jnp.int32, (HD, HD), 0) == lax.broadcasted_iota(
@@ -223,71 +223,25 @@
     def pair_at(region, n):
         return pl.ds(region * C + n * PAIR, PAIR)
 
-    def one_at(region, n, u):
-        return pl.ds(region * C + n * PAIR + u, 1)
-
-    def returns(n):
-        return (
-            remote(res.at[pair_at(1, n)], res.at[pair_at(5, n)], ret_ss, ret_rs, xl),
-            remote(res.at[pair_at(2, n)], res.at[pair_at(4, n)], ret_ss, ret_rs, xr),
-            remote(res.at[one_at(3, n, 0)], rel_r.at[pl.ds(n, 1)], ret_ss, rel_rs.at[0, n], xr),
-            remote(res.at[one_at(3, n, 1)], rel_l.at[pl.ds(n, 1)], ret_ss, rel_rs.at[1, n], xl),
-        )
-
-    def relays(n):
-        return (
-            remote(rel_r.at[pl.ds(n, 1)], res.at[one_at(6, n, 0)], fwd_ss, ret_rs, xr),
-            remote(rel_l.at[pl.ds(n, 1)], res.at[one_at(6, n, 1)], fwd_ss, ret_rs, xl),
-        )
-
-    def relay(n):
-        _, _, right, left = returns(n)
-        on_right, on_left = relays(n)
-        right.wait_recv()
-        on_right.start()
-        left.wait_recv()
-        on_left.start()
-
-    def step(n, carry):
-        @pl.when(n == 2)
-        def _():
-            for m, device in ((3, zr), (4, zl)):
-                k_to(m, kbuf.at[m], device).wait_recv()
-                k_to(m + 2, kbuf.at[m], device).start()
-
-        @pl.when(n == 3)
-        def _():
-            for m, device in ((3, zr), (4, zl)):
-                v_to(m, vbuf.at[m], device).wait_recv()
-                v_to(m + 2, vbuf.at[m], device).start()
-
-        @pl.when(n == 5)
-        def _():
-            k_to(5, kbuf.at[5], zr).wait_recv()
-            k_to(7, kbuf.at[5], zr).start()
-            k_to(6, kbuf.at[6], zl).wait_recv()
-            v_to(6, vbuf.at[6], zl).wait_recv()
-            v_to(7, vbuf.at[6], zl).start()
-            v_to(5, vbuf.at[5], zr).wait_recv()
-
-        @pl.when(n == 7)
-        def _():
-            k_to(7, kbuf.at[5], zr).wait_recv()
-            v_to(7, vbuf.at[6], zl).wait_recv()
-
+    homes = {1: (5, xl), 2: (4, xr), 3: (6, xx)}
+
+    def send_back(s, n):
+        region, device = homes[s]
+        remote(res.at[pair_at(s, n)], res.at[pair_at(region, n)], ret_ss, ret_rs, device).start()
+
+    def two_sources(n, sources):
         owner_z = (z + (1 - 2 * (n % 2)) * ((n + 1) // 2) + ZN) % ZN
         base = (x * ZN + owner_z) * PAIR
 
         def queries_of(s):
-            return jnp.concatenate(
-                [rows_of(qbuf[s * C + tabs[s, 0, base + u]]) for u in range(PAIR)], axis=0
-            )
-
-        scores[0] = scores_of(queries_of(0), kbuf[n])
-        for s in range(XN):
-            if s + 1 < XN:
-                scores[(s + 1) % 2] = scores_of(queries_of(s + 1), kbuf[n])
-            mixed, lse = soften(scores[s % 2], vbuf[n])
+            which = [tabs[s, 0, base + u] for u in range(PAIR)]
+            blocks = [qfar[w] if s == 3 else qbuf[s * C + w] for w in which]
+            return jnp.concatenate([rows_of(block) for block in blocks], axis=0)
+
+        for k, s in enumerate(sources):
+            scores[k] = scores_of(queries_of(s), kbuf[n])
+        for k, s in enumerate(sources):
+            mixed, lse = soften(scores[k], vbuf[n])
             mixed = mixed.astype(BF16)
             for u in range(PAIR):
                 here = s * C + n * PAIR + u
@@ -297,16 +251,53 @@
                 lsb[here] = jnp.sum(
                     jnp.where(eye, lse[u * HD : (u + 1) * HD], 0.0), axis=0, keepdims=True
                 )
-        for copy in returns(n):
-            copy.start()
-
-        @pl.when(n >= 2)
-        def _():
-            relay(n - 2)
+            if s:
+                send_back(s, n)
+
+    def step(h, carry):
+        @pl.when(h == 3)
+        def _():
+            remote(qfar, qfar, q_ss, q_rs.at[3], xl).wait_recv()
+
+        @pl.when(h == 4)
+        def _():
+            for m, device in ((3, zr), (4, zl)):
+                k_to(m, kbuf.at[m], device).wait_recv()
+                k_to(m + 2, kbuf.at[m], device).start()
+
+        @pl.when(h == 6)
+        def _():
+            for m, device in ((3, zr), (4, zl)):
+                v_to(m, vbuf.at[m], device).wait_recv()
+                v_to(m + 2, vbuf.at[m], device).start()
+
+        @pl.when(h == 8)
+        def _():
+            k_to(5, kbuf.at[5], zr).wait_recv()
+            k_to(7, kbuf.at[5], zr).start()
+            k_to(6, kbuf.at[6], zl).wait_recv()
+            v_to(6, vbuf.at[6], zl).wait_recv()
+            v_to(7, vbuf.at[6], zl).start()
+            v_to(5, vbuf.at[5], zr).wait_recv()
+
+        @pl.when(h == 10)
+        def _():
+            k_to(7, kbuf.at[5], zr).wait_recv()
+            v_to(7, vbuf.at[6], zl).wait_recv()
+
+        late_step = jnp.where(h < 3, 0, 1)
+
+        @pl.when(h >= 3)
+        def _():
+            two_sources(h - 3 * late_step, (3, 0))
+
+        @pl.when((h < 3) | (h >= 6))
+        def _():
+            two_sources(h - 3 * late_step, (1, 2))
 
         return carry
 
-    lax.fori_loop(0, ZN, step, 0)
+    lax.fori_loop(0, ZN + 3, step, 0)
     lse_copies = [
         remote(lsb.at[pl.ds(1 * C, C)], lsb.at[pl.ds(5 * C, C)], lse_ss, lse_rs, xl),
         remote(lsb.at[pl.ds(2 * C, C)], lsb.at[pl.ds(4 * C, C)], lse_ss, lse_rs, xr),
@@ -314,22 +305,23 @@
     ]
     for copy in lse_copies:
         copy.start()
-    relay(ZN - 2)
-    relay(ZN - 1)
 
     came = pl.ds(4 * C, 3 * C)
-    res_all = remote(res.at[came], res.at[came], fwd_ss, ret_rs, xl)
+    res_all = remote(res.at[came], res.at[came], ret_ss, ret_rs, xl)
     lse_all = remote(lsb.at[came], lsb.at[came], lse_ss, lse_rs, xl)
     res_all.wait_recv()
     lse_all.wait_recv()
 
-    def attn_copy(g):
+    def attn_copy(g, k):
         quarter = pl.ds(g * 4, 4)
-        return remote(attn.at[quarter], attn_sib.at[quarter], att_ss, att_rs, sibling)
-
-    def merge(g, carry):
-        for k in range(4):
-            c = g * 4 + k
+        return remote(
+            attn.at[quarter], attn_sib.at[quarter], att_ss, att_rs.at[(k + 2) // 3], sibling
+        )
+
+    def merge(k, carry):
+        g = (y + jnp.where(k == 0, 2, jnp.where(k == 1, 1, jnp.where(k == 2, 3, 0)))) % YN
+        for e in range(4):
+            c = g * 4 + e
             where = slot_s[c]
             prefix = rows_of(res[where]).astype(F32)
             prefix_lse = jnp.sum(jnp.where(eye, lsb[where], 0.0), axis=1, keepdims=True)
@@ -340,7 +332,7 @@
             joined = ((a * prefix + b * sfo[c]) / (a + b)).astype(BF16)
             for r in range(R):
                 attn[c, :, r * HD : (r + 1) * HD] = joined[r * L : (r + 1) * L]
-        attn_copy(g).start()
+        attn_copy(g, k).start()
         return carry
 
     lax.fori_loop(0, C // 4, merge, 0)
@@ -369,14 +361,26 @@
     def sib_copy(i):
         return remote(part.at[i, y, 1 - core], near.at[i, 4], sib_ss, near_rs.at[i], sibling)
 
-    def multiply(i):
-        summed = jnp.dot(
-            attn[...].reshape(C * L, R * HD), wbuf[0, i], preferred_element_type=F32
-        ) + jnp.dot(
-            attn_sib[...].reshape(C * L, R * HD), wbuf[1, i], preferred_element_type=F32
+    def product(i, chunks):
+        def rows(ref):
+            blocks = [ref[pl.ds(g * 4, 4)].reshape(4 * L, R * HD) for g in chunks]
+            return jnp.concatenate(blocks, axis=0)
+
+        summed = jnp.dot(rows(attn), wbuf[0, i], preferred_element_type=F32) + jnp.dot(
+            rows(attn_sib), wbuf[1, i], preferred_element_type=F32
         )
-        part[i] = summed.astype(BF16).reshape(YN, 2, ROWS, TILE)
-        for copy in far_copies(i) + now_copies(i) + (sib_copy(i),):
+        for e, g in enumerate(chunks):
+            block = summed[e * 4 * L : (e + 1) * 4 * L].astype(BF16)
+            part[i, g] = block.reshape(2, ROWS, TILE)
+
+    def multiply_far(i):
+        product(i, (far_at,))
+        for copy in far_copies(i):
+            copy.start()
+
+    def multiply_rest(i):
+        product(i, (yr_at, yl_at, y))
+        for copy in now_copies(i) + (sib_copy(i),):
             copy.start()
 
     def pass_on(i):
@@ -416,27 +420,38 @@
     pltpu.make_async_copy(wbuf.at[0], wbuf.at[0], w_sem).wait()
     w_all = remote(wbuf.at[1], wbuf.at[1], ws_ss, ws_rs, sibling)
     w_all.wait_recv()
-    attn_all = remote(attn, attn_sib, att_ss, att_rs, sibling)
-    attn_all.wait_recv()
+    attn_all = remote(attn, attn_sib, att_ss, att_rs.at[0], sibling)
+    attn_rest = remote(attn.at[pl.ds(0, 12)], attn_sib.at[pl.ds(0, 12)], att_ss, att_rs.at[1], sibling)
+    attn_copy(far_at, 0).wait_recv()
     res_copy.wait()
     head_copy.wait()
 
     def all_sent():
-        others, queries = pl.ds(1, ZN - 1), pl.ds(C, 3 * C)
+        others = pl.ds(1, ZN - 1)
         for copy in (
             remote(kbuf.at[others], kbuf.at[others], k_ss, k_rs.at[0], zr),
             remote(vbuf.at[others], vbuf.at[others], v_ss, v_rs.at[0], zr),
-            remote(qbuf.at[queries], qbuf.at[queries], q_ss, q_rs.at[0], xr),
-            remote(res.at[queries], res.at[queries], ret_ss, ret_rs, xr),
-            remote(res.at[pl.ds(0, C)], res.at[pl.ds(0, C)], fwd_ss, ret_rs, xr),
-            tab_all, lse_all, w_all, attn_all,
+            remote(qbuf, qbuf, q_ss, q_rs.at[0], xr),
+            tab_all, res_all, lse_all, w_all, attn_all,
         ):
             copy.wait_send()
 
     def tile_step(i, carry):
         @pl.when(i < TILES)
         def _():
-            multiply(i)
+            multiply_far(i)
+
+        @pl.when(i == TILES)
+        def _():
+            all_sent()
+
+        @pl.when(i == 1)
+        def _():
+            attn_rest.wait_recv()
+
+        @pl.when((i >= 1) & (i < TILES + 1))
+        def _():
+            multiply_rest(i - 1)
 
         @pl.when((i >= AHEAD) & (i < TILES + AHEAD))
         def _():
@@ -449,7 +464,6 @@
         return carry
 
     lax.fori_loop(0, TILES + BEHIND, tile_step, 0)
-    all_sent()
     tiles = near.at[:, pl.ds(0, 2)]
     for sem in (far_ss, now_ss, late_ss):
         remote(tiles, tiles, sem, near_rs.at[0], yr_same).wait_send()
@@ -481,7 +495,8 @@
         in_specs=[smem] * 3 + [any_space] * 8,
         out_specs=(vmem, vmem),
         scratch_shapes=[
-            pltpu.VMEM((XN * C, L, R * HD), BF16),
+            pltpu.VMEM((3 * C, L, R * HD), BF16),
+            pltpu.VMEM((C, L, R * HD), BF16),
             pltpu.VMEM((C * L, HD), BF16),
             pltpu.VMEM((C * L, HD), BF16),
             pltpu.VMEM((ZN, P_SIZE, HD), BF16),
@@ -490,8 +505,6 @@
             pltpu.SMEM((XN, 8, 128), jnp.int32),
             pltpu.VMEM((7 * C, L, R * HD), BF16),
             pltpu.VMEM((7 * C, 1, HD), F32),
-            pltpu.VMEM((ZN, L, R * HD), BF16),
-            pltpu.VMEM((ZN, L, R * HD), BF16),
             pltpu.VMEM((C, R * L, HD), F32),
             pltpu.VMEM((C, R * L, HD), F32),
             pltpu.SMEM((C,), jnp.int32),
@@ -506,9 +519,9 @@
             pltpu.VMEM((1, D), F32),
             pltpu.VMEM((ROWS, 128), F32),
             pltpu.VMEM((ROWS, 128), F32),
-            dma((8,)), dma, dma, dma, dma((3,)), dma, dma((ZN,)), dma, dma((ZN,)),
-            dma, dma, dma((2, ZN)), dma, dma, dma,
-            dma, dma, dma, dma, dma, dma, dma((TILES,)), dma, dma, dma, dma((TILES,)),
+            dma((8,)), dma, dma, dma, dma((4,)), dma, dma((ZN,)), dma, dma((ZN,)),
+            dma, dma, dma, dma,
+            dma, dma, dma, dma, dma((2,)), dma, dma((TILES,)), dma, dma, dma, dma((TILES,)),
         ],
         compiler_params=pltpu.CompilerParams(
             collective_id=0, has_side_effects=True, vmem_limit_bytes=VMEM_LIMIT

time: 102 us -> 99.4 us (0.975)
  Pallas kernels: 100 us -> 97.1 us
    pallas_call x1, Pallas kernels: 100 us -> 97.1 us  [fused(): pl.pallas_call(fused_kernel, out_shape=(pltpu.VMEM((ROWS, D), BF16), pltp...]
where the time goes in v4:
time: 99.4 us; the launch traced here: 99.3 us
  Pallas kernels  97.1 us (98%)
  local copies, waits for them, and re-layouts  1.53 us (2%)
    pallas_call x1, Pallas kernels, fused(): pl.pallas_call(fused_kernel, out_shape=(pltpu.VMEM((ROWS, D), BF16), pltp...  97.1 us

profile of v4, /device:TPU:1, one launch (start us, length us, event | category | flops | bytes accessed | tf_op | source)
XLA Modules:
  0.0 99.3 jit_solution(6099455529043926147)
XLA Ops:
  0.6 97.1 %shard_map.122 = (bf16[64,8192]{1,0:T(8,128)(2,1)S(1)}, f32[2,4]{1,0:T(2,128)S(1)}) custom-call(s32[16]{0:T(128)} %group_s.1, s32[16]{0:T(128)} %len_s.1, s32[4,16]{1,0:T(4,128)} %bitcast.5, bf16[16,32,512]{2,1,0:T(8,128)(2,1)} %bitcast.3, bf16[512,128]{1,0:T(8,128)(2,1)} %ck_in.1, bf16[512,128]{1,0:T(8,128)(2,1)} %cv_in.1, bf16[1024,128]{1,0:T(8,128)(2,1)} %pk.1, ...), custom_call_target="tpu_custom_call" | custom-call | flops 8589934592 | bytes 16777216 | tf_op jit(solution)/shard_map/pallas_call | solution.py:489
  97.7 1.0 copy.15
  98.7 0.6 copy.16

commit v5 on v4

--- a/solution.py
+++ b/solution.py
@@ -229,7 +229,7 @@
         region, device = homes[s]
         remote(res.at[pair_at(s, n)], res.at[pair_at(region, n)], ret_ss, ret_rs, device).start()
 
-    def two_sources(n, sources):
+    def form_scores(n, sources):
         owner_z = (z + (1 - 2 * (n % 2)) * ((n + 1) // 2) + ZN) % ZN
         base = (x * ZN + owner_z) * PAIR
 
@@ -240,6 +240,8 @@
 
         for k, s in enumerate(sources):
             scores[k] = scores_of(queries_of(s), kbuf[n])
+
+    def settle(n, sources):
         for k, s in enumerate(sources):
             mixed, lse = soften(scores[k], vbuf[n])
             mixed = mixed.astype(BF16)
@@ -254,6 +256,18 @@
             if s:
                 send_back(s, n)
 
+    def two_sources(n, sources):
+        form_scores(n, sources)
+        settle(n, sources)
+
+    def last_halves(buf, send_sem, recv_sems):
+        lower, upper = pl.ds(0, P_SIZE // 2), pl.ds(P_SIZE // 2, P_SIZE // 2)
+        last = recv_sems.at[ZN - 1]
+        return (
+            remote(buf.at[5, lower], buf.at[7, lower], send_sem, last, zr),
+            remote(buf.at[6, upper], buf.at[7, upper], send_sem, last, zl),
+        )
+
     def step(h, carry):
         @pl.when(h == 3)
         def _():
@@ -274,16 +288,13 @@
         @pl.when(h == 8)
         def _():
             k_to(5, kbuf.at[5], zr).wait_recv()
-            k_to(7, kbuf.at[5], zr).start()
             k_to(6, kbuf.at[6], zl).wait_recv()
+            for copy in last_halves(kbuf, k_ss, k_rs):
+                copy.start()
+            v_to(5, vbuf.at[5], zr).wait_recv()
             v_to(6, vbuf.at[6], zl).wait_recv()
-            v_to(7, vbuf.at[6], zl).start()
-            v_to(5, vbuf.at[5], zr).wait_recv()
-
-        @pl.when(h == 10)
-        def _():
-            k_to(7, kbuf.at[5], zr).wait_recv()
-            v_to(7, vbuf.at[6], zl).wait_recv()
+            for copy in last_halves(vbuf, v_ss, v_rs):
+                copy.start()
 
         late_step = jnp.where(h < 3, 0, 1)
 
@@ -297,7 +308,11 @@
 
         return carry
 
-    lax.fori_loop(0, ZN + 3, step, 0)
+    lax.fori_loop(0, ZN + 2, step, 0)
+    k_to(7, kbuf.at[7], zr).wait_recv()
+    form_scores(ZN - 1, (3, 1, 2, 0))
+    v_to(7, vbuf.at[7], zr).wait_recv()
+    settle(ZN - 1, (3, 1, 2, 0))
     lse_copies = [
         remote(lsb.at[pl.ds(1 * C, C)], lsb.at[pl.ds(5 * C, C)], lse_ss, lse_rs, xl),
         remote(lsb.at[pl.ds(2 * C, C)], lsb.at[pl.ds(4 * C, C)], lse_ss, lse_rs, xr),
@@ -508,7 +523,7 @@
             pltpu.VMEM((C, R * L, HD), F32),
             pltpu.VMEM((C, R * L, HD), F32),
             pltpu.SMEM((C,), jnp.int32),
-            pltpu.VMEM((2, PAIR * R * L, P_SIZE), F32),
+            pltpu.VMEM((XN, PAIR * R * L, P_SIZE), F32),
             pltpu.VMEM((C, L, R * HD), BF16),
             pltpu.VMEM((C, L, R * HD), BF16),
             pltpu.VMEM((2, TILES, R * HD, TILE), BF16),

time: 99.4 us -> 99.4 us (level)
  no operation moved by 1% of the time
where the time goes in v5:
time: 99.4 us; the launch traced here: 99.3 us
  Pallas kernels  97.1 us (98%)
  local copies, waits for them, and re-layouts  1.53 us (2%)
    pallas_call x1, Pallas kernels, fused(): pl.pallas_call(fused_kernel, out_shape=(pltpu.VMEM((ROWS, D), BF16), pltp...  97.1 us

profile of v5, /device:TPU:1, one launch (start us, length us, event | category | flops | bytes accessed | tf_op | source)
XLA Modules:
  0.0 99.3 jit_solution(12994948440375165211)
XLA Ops:
  0.6 97.1 %shard_map.122 = (bf16[64,8192]{1,0:T(8,128)(2,1)S(1)}, f32[2,4]{1,0:T(2,128)S(1)}) custom-call(s32[16]{0:T(128)} %group_s.1, s32[16]{0:T(128)} %len_s.1, s32[4,16]{1,0:T(4,128)} %bitcast.5, bf16[16,32,512]{2,1,0:T(8,128)(2,1)} %bitcast.3, bf16[512,128]{1,0:T(8,128)(2,1)} %ck_in.1, bf16[512,128]{1,0:T(8,128)(2,1)} %cv_in.1, bf16[1024,128]{1,0:T(8,128)(2,1)} %pk.1, ...), custom_call_target="tpu_custom_call" | custom-call | flops 8589934592 | bytes 16777216 | tf_op jit(solution)/shard_map/pallas_call | solution.py:504
  97.7 1.0 copy.15
  98.7 0.6 copy.16

commit v6 on v5

--- a/solution.py
+++ b/solution.py
@@ -285,34 +285,51 @@
                 v_to(m, vbuf.at[m], device).wait_recv()
                 v_to(m + 2, vbuf.at[m], device).start()
 
-        @pl.when(h == 8)
+        late_step = jnp.where(h < 3, 0, 1)
+
+        @pl.when(h >= 3)
+        def _():
+            two_sources(h - 3 * late_step, (3, 0))
+
+        @pl.when((h < 3) | (h >= 6))
+        def _():
+            two_sources(h - 3 * late_step, (1, 2))
+
+        return carry
+
+    lax.fori_loop(0, ZN, step, 0)
+
+    every = (3, 1, 2, 0)
+
+    def last_step(n, carry):
+        @pl.when(n == 5)
         def _():
             k_to(5, kbuf.at[5], zr).wait_recv()
             k_to(6, kbuf.at[6], zl).wait_recv()
             for copy in last_halves(kbuf, k_ss, k_rs):
                 copy.start()
+
+        @pl.when(n == 7)
+        def _():
+            k_to(7, kbuf.at[7], zr).wait_recv()
+
+        form_scores(n, every)
+
+        @pl.when(n == 5)
+        def _():
             v_to(5, vbuf.at[5], zr).wait_recv()
             v_to(6, vbuf.at[6], zl).wait_recv()
             for copy in last_halves(vbuf, v_ss, v_rs):
                 copy.start()
 
-        late_step = jnp.where(h < 3, 0, 1)
-
-        @pl.when(h >= 3)
-        def _():
-            two_sources(h - 3 * late_step, (3, 0))
-
-        @pl.when((h < 3) | (h >= 6))
-        def _():
-            two_sources(h - 3 * late_step, (1, 2))
-
+        @pl.when(n == 7)
+        def _():
+            v_to(7, vbuf.at[7], zr).wait_recv()
+
+        settle(n, every)
         return carry
 
-    lax.fori_loop(0, ZN + 2, step, 0)
-    k_to(7, kbuf.at[7], zr).wait_recv()
-    form_scores(ZN - 1, (3, 1, 2, 0))
-    v_to(7, vbuf.at[7], zr).wait_recv()
-    settle(ZN - 1, (3, 1, 2, 0))
+    lax.fori_loop(5, ZN, last_step, 0)
     lse_copies = [
         remote(lsb.at[pl.ds(1 * C, C)], lsb.at[pl.ds(5 * C, C)], lse_ss, lse_rs, xl),
         remote(lsb.at[pl.ds(2 * C, C)], lsb.at[pl.ds(4 * C, C)], lse_ss, lse_rs, xr),

time: 99.4 us -> 98.7 us (level)
  no operation moved by 1% of the time
where the time goes in v6:
time: 98.7 us; the launch traced here: 98.6 us
  Pallas kernels  96.4 us (98%)
  local copies, waits for them, and re-layouts  1.53 us (2%)
    pallas_call x1, Pallas kernels, fused(): pl.pallas_call(fused_kernel, out_shape=(pltpu.VMEM((ROWS, D), BF16), pltp...  96.4 us

profile of v6, /device:TPU:1, one launch (start us, length us, event | category | flops | bytes accessed | tf_op | source)
XLA Modules:
  0.0 98.6 jit_solution(3881821012473050927)
XLA Ops:
  0.6 96.4 %shard_map.122 = (bf16[64,8192]{1,0:T(8,128)(2,1)S(1)}, f32[2,4]{1,0:T(2,128)S(1)}) custom-call(s32[16]{0:T(128)} %group_s.1, s32[16]{0:T(128)} %len_s.1, s32[4,16]{1,0:T(4,128)} %bitcast.5, bf16[16,32,512]{2,1,0:T(8,128)(2,1)} %bitcast.3, bf16[512,128]{1,0:T(8,128)(2,1)} %ck_in.1, bf16[512,128]{1,0:T(8,128)(2,1)} %cv_in.1, bf16[1024,128]{1,0:T(8,128)(2,1)} %pk.1, ...), custom_call_target="tpu_custom_call" | custom-call | flops 8589934592 | bytes 16777216 | tf_op jit(solution)/shard_map/pallas_call | solution.py:521
  97.1 1.0 copy.15
  98.0 0.6 copy.16
